TPU v7x, 32 devices: a whole 2x2x4 slice. The times are simulated.
32 devices in a mesh: groups: 2 (over x), seq: 8 (over z, y), tp: 2 (over core).
Axes of the slice: x: 2, y: 2, z: 4, core: 2. Of those that a mesh axis runs over, the one named last changes fastest.
Arguments:
- queries: bfloat16 [16384, 4096], P(('groups', 'seq'), 'tp'), parts along dimension 0, may hold values from -6 to 6
- keys: bfloat16 [16384, 4096], P(('groups', 'seq'), 'tp'), parts along dimension 0, may hold values from -6 to 6
- values: bfloat16 [16384, 4096], P(('groups', 'seq'), 'tp'), parts along dimension 0, may hold values from -6 to 6
- log_decay: float32 [16384, 32], P(('groups', 'seq'), 'tp'), parts along dimension 0, may hold values from -1 to 0, as said below
- gate: bfloat16 [16384, 4096], P(('groups', 'seq'), 'tp'), parts along dimension 0, may hold values from -6 to 6
- gain: bfloat16 [4096], P('tp'), may hold values from 0.099609375 to 1.8984375
- doc_lengths: int32 [16], P('groups'), parts along dimension 0, may hold values from 1 to 4096, 8192 in all
- owner_ids: int32 [16], P('groups'), parts along dimension 0, may hold values from 0 to 7, each once
Outputs:
- mixed: bfloat16 [16384, 4096], P(('groups', 'seq'), 'tp'), parts along dimension 0
- owner_states: bfloat16 [16, 32, 128, 128], P(('groups', 'seq'), 'tp'), parts along dimension 0
There are 2 independent parts, one for each index of `groups`. A program takes and returns all parts, laid end to end along the dimension named above; an argument that names none is the same for every part. Nothing has to cross between parts.
Inputs may be any that keep to these rules, and one draw needn't show every extreme that they name: `doc_lengths`: positive lengths summing to 8192; the longest prompt has exactly 4096 tokens. `owner_ids`: a permutation of the owner slots. `log_decay`: negative.
All inputs are finite; a program needn't handle non-finite values.
Results may differ from a plain program's by a relative error of at most 0.0049.
Values may be sent and summed in bfloat16 or wider, within the bound.
No kernel may reach another device: no remote copies, remote signals or barrier semaphores. Data moves between devices by JAX's collectives and lax.ppermute only.
A program may use at most 192 MiB of HBM per device.

v0:
```python
import jax
import jax.numpy as jnp
from jax import lax
from jax.sharding import PartitionSpec as P

BLK = 512


highest_prec = lax.Precision.HIGHEST


def entering(part, axis, combine, identity):
    place = lax.axis_index(axis)
    gathered = jax.tree.map(lambda a: lax.all_gather(a, axis), part)
    state = jax.tree.map(lambda a, e: jnp.zeros_like(a) + jnp.asarray(e, a.dtype), part, identity)

    def one(step, state):
        return combine(
            state, jax.tree.map(lambda a: lax.dynamic_index_in_dim(a, step, 0, False), gathered)
        )

    return lax.fori_loop(0, place, one, state)


def local_intra(query_part, key_part, value_part, decay_part, seg_part, key_scale):
    index_row = jnp.arange(seg_part.shape[0], dtype=jnp.int32)
    causal = (index_row[None, :] <= index_row[:, None]) & (seg_part[:, None] == seg_part[None, :])
    scores = (
        jnp.einsum("ihd,jhd->hij", query_part, key_part, preferred_element_type=jnp.float32)
        * key_scale
    )
    cum_heads = decay_part.T
    exponent = jnp.where(causal[None], cum_heads[:, :, None] - cum_heads[:, None, :], -1e30)
    weights = (scores * jnp.exp(exponent)).astype(jnp.bfloat16)
    return jnp.einsum("hij,jhd->ihd", weights, value_part, preferred_element_type=jnp.float32)


def local_state(carried, key_part, value_part, decay_part, seg_part, prev_seg, key_scale):
    last_cum = decay_part[-1]
    same_doc = (seg_part == seg_part[-1]).astype(jnp.float32)
    weighted = (
        key_part.astype(jnp.float32)
        * key_scale
        * jnp.exp(last_cum[None, :] - decay_part)[:, :, None]
        * same_doc[:, None, None]
    )
    weighted = weighted.astype(jnp.bfloat16)
    no_reset = (seg_part[-1] == prev_seg).astype(jnp.float32)
    outer_sum = jnp.einsum("jhd,jhe->hde", weighted, value_part, preferred_element_type=jnp.float32)
    return (jnp.exp(last_cum) * no_reset)[:, None, None] * carried + outer_sum


def link_states(earlier, later):
    return (earlier[0] * later[0], later[0][:, None, None] * earlier[1] + later[1])


def on_device(queries, keys, values, log_decay, gate, gain, doc_lengths, owner_ids):
    row_count = queries.shape[0]
    heads_local = log_decay.shape[1]
    head_dim = queries.shape[1] // heads_local
    key_scale = head_dim ** (-0.5)
    nblock = row_count // BLK
    doc_count = owner_ids.shape[0]
    device = lax.axis_index("seq")
    first_row = device * row_count
    doc_ends = jnp.cumsum(doc_lengths)
    positions = first_row + jnp.arange(row_count, dtype=jnp.int32)
    segment = jnp.sum((positions[:, None] >= doc_ends[None, :]).astype(jnp.int32), axis=1)
    seg_start = jnp.sum((first_row - 1 >= doc_ends).astype(jnp.int32))
    segment_blk = segment.reshape(nblock, BLK)
    seg_before = jnp.concatenate([seg_start[None], segment_blk[:-1, -1]])
    query_blk = queries.reshape(nblock, BLK, heads_local, head_dim)
    key_blk = keys.reshape(nblock, BLK, heads_local, head_dim)
    value_blk = values.reshape(nblock, BLK, heads_local, head_dim)
    cum_decay = jnp.cumsum(log_decay.reshape(nblock, BLK, heads_local), axis=1)

    def advance(carried, inputs):
        query_part, key_part, value_part, decay_part, seg_part, prev_seg = inputs
        intra = local_intra(query_part, key_part, value_part, decay_part, seg_part, key_scale)
        updated = local_state(
            carried, key_part, value_part, decay_part, seg_part, prev_seg, key_scale
        )
        return (updated, (intra, carried))

    state_zero = jnp.zeros((heads_local, head_dim, head_dim), jnp.float32)
    local_end, (intra_all, starts_local) = lax.scan(
        advance, state_zero, (query_blk, key_blk, value_blk, cum_decay, segment_blk, seg_before)
    )
    block_totals = cum_decay[:, -1, :]
    before_sum = jnp.cumsum(block_totals, axis=0) - block_totals
    reach = (seg_before == seg_start).astype(jnp.float32)
    lead_rate = jnp.exp(before_sum) * reach[:, None]
    span_rate = jnp.exp(jnp.sum(block_totals, axis=0)) * (segment_blk[-1, -1] == seg_start).astype(
        jnp.float32
    )
    identity = (jnp.ones((heads_local,), jnp.float32), state_zero)
    _, incoming = entering((span_rate, local_end), "seq", link_states, identity)
    starts_global = starts_local + lead_rate[:, :, None, None] * incoming[None]
    keep_carry = (segment_blk == seg_before[:, None]).astype(jnp.float32)
    carry_weight = jnp.exp(cum_decay) * keep_carry[:, :, None]
    inter = jnp.einsum(
        "nihd,nhde->nihe", query_blk.astype(jnp.float32), starts_global, precision=highest_prec
    )
    attended = (intra_all + inter * carry_weight[:, :, :, None]).reshape(
        row_count, heads_local, head_dim
    )
    square_mean = jnp.mean(attended * attended, axis=-1, keepdims=True)
    gate_part = jax.nn.sigmoid(gate.reshape(row_count, heads_local, head_dim).astype(jnp.float32))
    gain_part = gain.reshape(heads_local, head_dim).astype(jnp.float32)
    mixed = (
        (attended * lax.rsqrt(square_mean + 1e-06) * gain_part[None] * gate_part)
        .reshape(row_count, -1)
        .astype(jnp.bfloat16)
    )

    def finish(doc_index):
        end_local = doc_ends[doc_index] - 1 - first_row
        present = (end_local >= 0) & (end_local < row_count)
        clipped = jnp.clip(end_local, 0, row_count - 1)
        block_index = clipped // BLK
        inner_index = clipped - block_index * BLK

        def pick(source):
            return lax.dynamic_index_in_dim(source, block_index, 0, keepdims=False)

        def compute(unused):
            decay_part = pick(cum_decay)
            seg_part = pick(segment_blk)
            index_row = jnp.arange(BLK, dtype=jnp.int32)
            end_decay = lax.dynamic_index_in_dim(decay_part, inner_index, 0, keepdims=False)
            taken = (index_row <= inner_index) & (seg_part == doc_index)
            exponent = jnp.where(taken[:, None], end_decay[None, :] - decay_part, -1e30)
            weighted = (
                pick(key_blk).astype(jnp.float32) * key_scale * jnp.exp(exponent)[:, :, None]
            ).astype(jnp.bfloat16)
            entry_rate = jnp.exp(end_decay) * jnp.where(pick(seg_before) == doc_index, 1.0, 0.0)
            outer_sum = jnp.einsum(
                "jhd,jhe->hde", weighted, pick(value_blk), preferred_element_type=jnp.float32
            )
            return (entry_rate[:, None, None] * pick(starts_global) + outer_sum).astype(
                jnp.bfloat16
            )

        def absent(unused):
            return jnp.zeros((heads_local, head_dim, head_dim), jnp.bfloat16)

        return lax.cond(present, compute, absent, 0)

    finals = lax.map(finish, jnp.arange(doc_count, dtype=jnp.int32))
    owner_table = (owner_ids[None, :] == jnp.arange(doc_count, dtype=jnp.int32)[:, None]).astype(
        jnp.bfloat16
    )
    ordered = jnp.einsum(
        "od,dhxy->ohxy", owner_table, finals, preferred_element_type=jnp.float32
    ).astype(jnp.bfloat16)
    received = lax.all_to_all(ordered, "seq", split_axis=0, concat_axis=0, tiled=True)
    owned = jnp.sum(received.astype(jnp.float32), axis=0, keepdims=True).astype(jnp.bfloat16)
    return (mixed, owned)


def solution(mesh):
    placed = (
        P(("groups", "seq"), "tp"),
        P(("groups", "seq"), "tp"),
        P(("groups", "seq"), "tp"),
        P(("groups", "seq"), "tp"),
        P(("groups", "seq"), "tp"),
        P("tp"),
        P("groups"),
        P("groups"),
    )
    return jax.shard_map(
        on_device,
        mesh=mesh,
        in_specs=placed,
        out_specs=(P(("groups", "seq"), "tp"), P(("groups", "seq"), "tp", None, None)),
        check_vma=False,
    )
```

profile of v0, /device:TPU:0, one launch (start us, length us, event | category | flops | bytes accessed | tf_op | source)
XLA Modules:
  0.0 392.8 jit_solution(12027594440588343124)
XLA Ops:
  7.3 0.8 reduce-window.20
  8.9 0.7 fusion.67
  9.6 0.8 copy_bitcast_fusion.4
  10.4 2.3 reduce-window.18
  13.0 3.6 copy.113
  16.6 3.1 copy.91
  19.6 1.4 copy.114
  21.1 3.1 copy.92
  24.2 1.0 copy-done
  25.2 1.0 copy-done.4
  26.2 3.4 copy.112
  29.6 2.5 compare_convert_fusion.2
  32.0 47.0 %while.42 = (s32[]{:T(128)}, f32[16,128,128]{2,1,0:T(8,128)S(1)}, f32[2,512,16,128]{1,3,2,0:T(8,128)}, f32[2,16,128,128]{3,2,1,0:T(8,128)}, f32[2,512,16]{1,2,0:...) while((s32[]{:T(128)}, f32[16,128,128]{2,1,0:T(8,128)S(1)}, ...), condition=%wide.region_6.7_spmd.clone, body=%wide.region_5.6_spmd.clone.sunk | while | flops 2442937344 | bytes 23837784 | solution.py:86
  32.9 2.0 constant_dynamic-slice_fusion.5
  34.9 11.7 %bitcast_dynamic-update-slice_fusion.4 = f32[2,512,16,128]{1,3,2,0:T(8,128)} fusion(f32[2,512,16,128]{1,3,2,0:T(8,128)} %get-tuple-element.826, s32[]{:T(128)} %get-tuple-element.824, f32[16,512]{1,0:T(8,128)} %dynamic-slice_bitcast_fusion.5, pred[512,512]{1,0:T(8,128)(4,1)S(1)} %fusion.82, bf16[2,512,16,128]{3,1,2,0:T(8,128)(2,1)} %get-tuple-element.846, ...), kind=kOutput, calls=%fused_computation.26.clone.1 | convolution fusion | flops 2168455168 | bytes 10814976 | tf_op jit(solution)/shard_map/while/body/eval_jaxpr/hij,jhd->ihd/dot_general | solution.py:35
  50.0 1.1 bitcast_dynamic-update-slice_fusion.5
  51.1 4.4 %fusion.81 = f32[16,128,128]{2,1,0:T(8,128)S(1)} fusion(bf16[2,512,16,128]{3,1,2,0:T(8,128)(2,1)} %get-tuple-element.845, s32[]{:T(128)} %get-tuple-element.824, f32[512]{0:T(512)S(1)} %compare_convert_fusion.5, f32[512,16]{0,1:T(8,128)S(1)} %fusion.80, bf16[1,512,16,128]{3,2,1,0:T(8,128)(2,1)S(1)} %constant_dynamic-slice_fusion.5, ...), kind=kOutput, calls=%fused_computation.39.clone.1 | convolution fusion | flops 273416192 | bytes 6326849 | tf_op jit(solution)/shard_map/while/body/eval_jaxpr/jhd,jhe->hde/dot_general | solution.py:49
  56.4 2.0 constant_dynamic-slice_fusion.5
  58.3 11.7 %bitcast_dynamic-update-slice_fusion.4 = f32[2,512,16,128]{1,3,2,0:T(8,128)} fusion(f32[2,512,16,128]{1,3,2,0:T(8,128)} %get-tuple-element.826, s32[]{:T(128)} %get-tuple-element.824, f32[16,512]{1,0:T(8,128)} %dynamic-slice_bitcast_fusion.5, pred[512,512]{1,0:T(8,128)(4,1)S(1)} %fusion.82, bf16[2,512,16,128]{3,1,2,0:T(8,128)(2,1)} %get-tuple-element.846, ...), kind=kOutput, calls=%fused_computation.26.clone.1 | convolution fusion | flops 2168455168 | bytes 10814976 | tf_op jit(solution)/shard_map/while/body/eval_jaxpr/hij,jhd->ihd/dot_general | solution.py:35
  73.6 1.1 bitcast_dynamic-update-slice_fusion.5
  74.6 4.4 %fusion.81 = f32[16,128,128]{2,1,0:T(8,128)S(1)} fusion(bf16[2,512,16,128]{3,1,2,0:T(8,128)(2,1)} %get-tuple-element.845, s32[]{:T(128)} %get-tuple-element.824, f32[512]{0:T(512)S(1)} %compare_convert_fusion.5, f32[512,16]{0,1:T(8,128)S(1)} %fusion.80, bf16[1,512,16,128]{3,2,1,0:T(8,128)(2,1)S(1)} %constant_dynamic-slice_fusion.5, ...), kind=kOutput, calls=%fused_computation.39.clone.1 | convolution fusion | flops 273416192 | bytes 6326849 | tf_op jit(solution)/shard_map/while/body/eval_jaxpr/jhd,jhe->hde/dot_general | solution.py:49
  79.0 1.0 copy-done.1
  80.1 7.6 %copy.98 = bf16[2,512,16,128]{1,3,2,0:T(8,128)(2,1)} copy(bf16[2,512,16,128]{3,2,1,0:T(8,128)(2,1)} %get-tuple-element.924) | data formatting | bytes 8388608 | tf_op jit(solution)/shard_map/while | solution.py:149
  90.7 23.7 %all-reduce = f32[128]{0:T(128)S(1)} all-reduce(f32[128]{0:T(128)S(1)} %multiply_dynamic-update-slice_fusion), channel_id=2, replica_groups=mesh['groups'=2,'seq'=8,'tp'=2] {'seq'}, use_global_device_ids=true, to_apply=%add | all-reduce | flops 128 | bytes 1024
  114.6 93.5 %all-gather.4.cloned.1.call-done = f32[128,128,128]{2,1,0:T(8,128)} async-done(((f32[16,128,128]{2,1,0:T(8,128)}), f32[128,128,128]{2,1,0:T(8,128)}) %all-gather.4.cloned.1.call-update) | async-done | bytes 8388624 | tf_op jit(solution)/shard_map/all_gather | solution.py:14
  208.2 1.8 multiply_add_fusion
  210.1 45.8 %while.41 = (s32[]{:T(128)}, bf16[8,16,128,128]{3,2,1,0:T(8,128)(2,1)}, s32[8]{0:T(128)S(1)}, s32[8]{0:T(128)S(1)}, s32[]{:T(128)}, /*index=5*/f32[2,512,16]{1,2...) while((s32[]{:T(128)}, ...), condition=%wide.region_15.16_spmd, body=%wide.region_12.15_spmd.sunk | while | flops 272393760 | bytes 6921193 | solution.py:149
  214.1 6.0 %conditional.2 = (bf16[1,16,128,128]{3,2,1,0:T(8,128)(2,1)S(1)}) conditional(s32[]{:T(128)} %convert_element_type.161, () %tuple.109, (s32[]{:T(128)}, f32[2,512,16]{1,2,0:T(8,128)S(1)}, s32[2]{0:T(128)S(1)}, s32[]{:T(128)}, f32[2,16,128,128]{3,2,1,0:T(8,128)S(1)}, /*index=5*/bf16[2,512,16,128]{1,3,2,0:T(8,128)(2,1)}, s32[2,512]{1,0:T(2,128)S(1)}, ...), branch_computations={%region_13.13_spmd, %region_14.14_spmd} | conditional | flops 272393760 | bytes 5871784 | solution.py:147
  214.2 0.7 compare_reduce_fusion
  217.2 2.9 fusion.18
  220.1 0.8 constant_dynamic-update-slice_fusion.2
  225.1 0.8 constant_dynamic-update-slice_fusion.2
  230.1 0.8 constant_dynamic-update-slice_fusion.2
  235.1 0.8 constant_dynamic-update-slice_fusion.2
  240.1 0.8 constant_dynamic-update-slice_fusion.2
  245.1 0.8 constant_dynamic-update-slice_fusion.2
  250.1 0.8 constant_dynamic-update-slice_fusion.2
  255.1 0.8 constant_dynamic-update-slice_fusion.2
  255.9 4.7 %fusion.61 = bf16[8,16,128,128]{3,0,2,1:T(8,128)(2,1)S(1)} fusion(bf16[8,16,128,128]{3,2,1,0:T(8,128)(2,1)} %get-tuple-element.431, s32[8]{0:T(128)S(1)} %copy-done.7), kind=kOutput, calls=%fused_computation.65 | convolution fusion | flops 35651648 | bytes 8388640 | tf_op jit(solution)/shard_map/od,dhxy->ohxy/dot_general | solution.py:153
  260.6 3.1 copy.101
  263.7 24.9 %all-to-all-start = ((bf16[8,16,128,128]{3,2,1,0:T(8,128)(2,1)}), bf16[8,16,128,128]{3,2,1,0:T(8,128)(2,1)}, u32[]{:S(2)}, u32[]{:S(2)}) async-start(bf16[8,16,128,128]{3,2,1,0:T(8,128)(2,1)} %copy.101), calls=%async_computation | async-start | bytes 8388608 | tf_op jit(solution)/shard_map/all_to_all | solution.py:156
  288.8 13.5 %multiply_reduce_fusion = (f32[2,512,16]{1,2,0:T(8,128)S(1)}, f32[2,512,16,128]{1,3,2,0:T(8,128)}) fusion(f32[2,512,16,128]{1,3,2,0:T(8,128)} %get-tuple-element.427, f32[2,512,16]{1,2,0:T(8,128)S(1)} %exponential_multiply_fusion.2, f32[2,16,128,128]{3,2,1,0:T(8,128)S(1)} %get-tuple-element.929, bf16[2,512,16,128]{3,2,1,0:T(8,128)(2,1)} %bitcast.182), kind=kOutput, calls=%fused_computation.62 | convolution fusion | flops 3229597696 | bytes 23199744 | tf_op jit(solution)/shard_map/nihd,nhde->nihe/dot_general | solution.py:101
  302.5 10.3 %copy.95 = f32[2,512,16,128]{3,2,1,0:T(8,128)} copy(f32[2,512,16,128]{1,3,2,0:T(8,128)} %get-tuple-element.650) | data formatting | bytes 16777216 | tf_op jit(solution)/shard_map/add | solution.py:104
  312.8 2.3 mul.220
  315.1 1.1 copy-done.2
  316.2 12.3 %fusion.57 = bf16[1024,2048]{1,0:T(8,128)(2,1)} fusion(f32[128,8,16,128]{3,2,1,0:T(8,128)S(1)} %bitcast.184, f32[128,8,16,128]{3,2,1,0:T(8,128)S(1)} %bitcast.183, bf16[1024,2048]{1,0:T(8,128)(2,1)} %param.20, f32[2048]{0:T(1024)S(1)} %convert_element_type.110), kind=kLoop, calls=%fused_computation.59 | loop fusion | flops 16777216 | bytes 25174016 | tf_op jit(solution)/shard_map/convert_element_type | solution.py:113
  328.5 53.6 %all-to-all-done = bf16[8,16,128,128]{3,2,1,0:T(8,128)(2,1)} async-done(((bf16[8,16,128,128]{3,2,1,0:T(8,128)(2,1)}), bf16[8,16,128,128]{3,2,1,0:T(8,128)(2,1)}, u32[]{:S(2)}, u32[]{:S(2)}) %all-to-all-start) | async-done | bytes 4194336 | tf_op jit(solution)/shard_map/all_to_all | solution.py:156
  382.1 3.8 reduce_sum.52
  (100 shorter events, 21.9 us)
Async XLA Ops:
  7.2 200.9 %all-gather.4.cloned.1.call-start = ((), (), s32[]{:S(2)}) async-start(), calls=%async_computation.1 | async-start | bytes 9437184 | tf_op jit(solution)/shard_map/all_gather | solution.py:14
  8.1 1.5 copy-start.8
  16.6 3.1 copy-start.3
  21.1 4.1 %copy-start = (bf16[128,8,16,128]{3,2,1,0:T(8,128)(2,1)}, bf16[128,8,16,128]{3,2,1,0:T(8,128)(2,1)S(1)}, u32[]{:S(2)}) copy-start(bf16[128,8,16,128]{3,2,1,0:T(8,128)(2,1)S(1)} %copy.114) | copy-start | bytes 12582916
  21.1 5.1 %copy-start.4 = (bf16[1024,2048]{1,0:T(8,128)(2,1)S(1)}, bf16[1024,2048]{1,0:T(8,128)(2,1)}, u32[]{:S(2)}) copy-start(bf16[1024,2048]{1,0:T(8,128)(2,1)} %param.17) | copy-start | bytes 12582916
  79.0 1.0 copy-start.1
  80.0 8.9 %copy-start.10 = (u32[32]{0:T(128)S(1)}, u32[32]{0:T(128)}, u32[]{:S(2)}) copy-start(u32[32]{0:T(128)} %constant.247) | copy-start | bytes 388
  80.0 34.5 %copy-start.6 = (f32[2]{0:T(128)S(1)}, f32[2]{0:T(128)}, u32[]{:S(2)}) copy-start(f32[2]{0:T(128)} %get-tuple-element.645) | copy-start | bytes 28
  208.2 1.9 copy-start.9
  210.1 45.9 %copy-start.7 = (s32[8]{0:T(128)S(1)}, s32[8]{0:T(128)}, u32[]{:S(2)}) copy-start(s32[8]{0:T(128)} %param.23) | copy-start | bytes 100
  263.7 24.9 %copy-start.5 = (bf16[2048]{0:T(1024)(128)(2,1)S(1)}, bf16[2048]{0:T(1024)(128)(2,1)}, u32[]{:S(2)}) copy-start(bf16[2048]{0:T(1024)(128)(2,1)} %param.21) | copy-start | bytes 12292
  263.7 118.4 %all-to-all-start = ((bf16[8,16,128,128]{3,2,1,0:T(8,128)(2,1)}), bf16[8,16,128,128]{3,2,1,0:T(8,128)(2,1)}, u32[]{:S(2)}, u32[]{:S(2)}) async-start(bf16[8,16,128,128]{3,2,1,0:T(8,128)(2,1)} %copy.101), calls=%async_computation | async-start | bytes 8388608 | tf_op jit(solution)/shard_map/all_to_all | solution.py:156
  312.8 3.4 copy-start.2
Sparse Core Ops, SparseCore 0:
  80.1 127.9 all-gather.3
where the time goes:
time: 397 us; the launch traced here: 393 us
  waiting for transfers between devices  147 us (37%)
  local copies, waits for them, and re-layouts  71.2 us (18%)
  matrix products  53.4 us (13%)
  other arithmetic  30.1 us (8%)
  loops' own time  26.1 us (7%)
  starting transfers between devices  24.9 us (6%)
  blocking collectives  23.7 us (6%)
  between operations  16.3 us (4%)
    all_gather x1, waiting for transfers between devices, entering(): gathered = jax.tree.map(lambda a: lax.all_gather(a, axis), part)  93.5 us
    all_to_all x1, waiting for transfers between devices, on_device(): lax.all_to_all(ordered, 'seq', split_axis=0, concat_axis=0, tiled=True)  53.6 us
    all_to_all x1, starting transfers between devices, on_device(): lax.all_to_all(ordered, 'seq', split_axis=0, concat_axis=0, tiled=True)  24.9 us
    unnamed x1, blocking collectives  23.7 us
    dot_general x2, matrix products, local_intra(): jnp.einsum('hij,jhd->ihd', weights, value_part, preferred_element_type=jn...  23.4 us
    another operation x1, loops' own time, on_device(): finals = lax.map(finish, jnp.arange(doc_count, dtype=jnp.int32))  21.9 us
    unnamed x29, local copies, waits for them, and re-layouts  19.3 us
    dot_general x1, matrix products, on_device(): jnp.einsum('nihd,nhde->nihe', query_blk.astype(jnp.float32), starts_globa...  13.5 us
  transfers between devices with their start and end apart: 2, of which 2 were waited for; matrix products, arithmetic and copies ran while one was open for 12% of the time, Pallas kernels for 0%

commit v1 on v0

v1 whole, which is shorter than its diff:
```python
import functools
import math

import jax
import jax.numpy as jnp
from jax import lax
from jax.experimental import pallas as pl
from jax.experimental.pallas import tpu as pltpu
from jax.sharding import PartitionSpec as P

BLK = 512
SIDE = 3
EXTRA = 16
NEG = -1e30
LOG2E = math.log2(math.e)
F32, BF16 = jnp.float32, jnp.bfloat16


def dot(a, b, contract=((1,), (0,))):
    return lax.dot_general(a, b, (contract, ((), ())), preferred_element_type=F32)


def iota(shape, dim):
    return lax.broadcasted_iota(jnp.int32, shape, dim)


def read_ends(len_ref, count):
    ends, total = [], jnp.int32(0)
    for d in range(count):
        total = total + len_ref[d]
        ends.append(total)
    return ends


def run_end(ends, pos):
    best = ends[-1]
    for e in reversed(ends[:-1]):
        best = jnp.where(e > pos, e, best)
    return best


def run_start(ends, pos):
    best = jnp.zeros_like(pos)
    for e in ends[:-1]:
        best = jnp.where(e <= pos, e, best)
    return best


def split3(x):
    hi = x.astype(BF16)
    rest = x - hi.astype(F32)
    mid = rest.astype(BF16)
    return hi, mid, (rest - mid.astype(F32)).astype(BF16)


def fill_cums(ld_ref, crow_ref, ccol_ref):
    heads, rows = ld_ref.shape
    upper = (iota((BLK, BLK), 0) <= iota((BLK, BLK), 1)).astype(F32).astype(BF16)
    lower = (iota((BLK, BLK), 0) >= iota((BLK, BLK), 1)).astype(F32).astype(BF16)
    base_row = jnp.zeros((heads, 1), F32)
    base_col = jnp.zeros((1, heads), F32)
    for b in range(rows // BLK):
        part = ld_ref[:, b * BLK : (b + 1) * BLK] * LOG2E
        row = jnp.zeros((heads, BLK), F32)
        col = jnp.zeros((BLK, heads), F32)
        for piece in reversed(split3(part)):
            row = row + dot(piece, upper)
            col = col + dot(lower, piece, ((1,), (1,)))
        row, col = row + base_row, col + base_col
        crow_ref[:, b * BLK : (b + 1) * BLK] = row
        ccol_ref[b * BLK : (b + 1) * BLK, :] = col
        base_row, base_col = row[:, BLK - 1 :], col[BLK - 1 :, :]


def pieces_kernel(scale, slots, by_owner, len_ref, own_ref, ld_ref, k_ref, v_ref, out_ref, *rest):
    heads, rows = ld_ref.shape
    count = len_ref.shape[0]
    if by_owner:
        crow_ref, ccol_ref, w_ref = rest
        first_ref = None
    else:
        crow_ref, ccol_ref, w_ref, first_ref = rest
    step = pl.program_id(0)
    hp = k_ref.shape[1] // 128

    @pl.when(step == 0)
    def _():
        fill_cums(ld_ref, crow_ref, ccol_ref)
        first = lax.axis_index("seq") * rows
        last = first + rows - 1
        ends = read_ends(len_ref, count)
        starts = [jnp.int32(0)] + ends[:-1]
        lows = [jnp.int32(0)] * slots
        highs = [jnp.int32(-1)] * slots
        place = jnp.int32(0)
        for d in range(count):
            here = (ends[d] > first) & (ends[d] <= last)
            low = jnp.maximum(starts[d] - first, 0)
            high = ends[d] - 1 - first
            for s in range(slots):
                if by_owner:
                    mine = here & (place >= SIDE) & (own_ref[d] == s)
                else:
                    mine = here & (place == s - 1)
                lows[s] = jnp.where(mine, low, lows[s])
                highs[s] = jnp.where(mine, high, highs[s])
            place = place + here.astype(jnp.int32)
        if not by_owner:
            lows[0] = jnp.maximum(run_start(ends, last) - first, 0)
            highs[0] = jnp.int32(rows - 1)
        at = iota((heads, rows), 1)
        cum = crow_ref[...]
        for s in range(slots):
            end_cum = jnp.sum(jnp.where(at == highs[s], cum, 0.0), axis=1, keepdims=True)
            inside = (at >= lows[s]) & (at <= highs[s])
            w_ref[s] = jnp.exp2(jnp.where(inside, end_cum - cum, NEG) + math.log2(scale))
        if not by_owner:
            stop = jnp.minimum(run_end(ends, first) - 1 - first, rows - 1)
            goes_on = (run_start(ends, first) < first).astype(F32)
            stop_cum = jnp.sum(jnp.where(at == stop, cum, 0.0), axis=1, keepdims=True)
            first_ref[...] = jnp.broadcast_to(jnp.exp2(stop_cum) * goes_on, (heads, 128))

    for i in range(hp):
        h = step * hp + i
        flipped = k_ref[:, i * 128 : (i + 1) * 128].astype(F32).T
        value = v_ref[:, i * 128 : (i + 1) * 128]
        for s in range(slots):
            weighted = (flipped * w_ref[s, pl.ds(h, 1), :]).astype(BF16)
            state = dot(weighted, value).astype(BF16)
            if by_owner:
                out_ref[s, i] = state
            else:
                at = (s * hp + i) * 128
                out_ref[0, at : at + 128, :] = state
    if not by_owner:
        rate = first_ref[pl.ds(step * hp, hp), :]
        high = rate.astype(BF16).astype(F32)
        pad = jnp.zeros((EXTRA // 2 - hp, 128), F32)
        tail = jnp.concatenate([high, pad, rate - high, pad], axis=0) if hp < EXTRA // 2 else jnp.concatenate([high, rate - high], axis=0)
        out_ref[0, slots * hp * 128 :, :] = tail.astype(BF16)


def piece_states(doc_lengths, owner_ids, decay_rows, keys, values, spread, slots, by_owner):
    heads, rows = decay_rows.shape
    hp = heads // spread
    whole = lambda shape: pl.BlockSpec(shape, lambda j: (0,) * len(shape))
    smem = pl.BlockSpec(memory_space=pltpu.SMEM)
    wide = pl.BlockSpec((rows, hp * 128), lambda j: (0, j))
    if by_owner:
        out = jax.ShapeDtypeStruct((slots, heads, 128, 128), BF16)
        out_spec = pl.BlockSpec((slots, hp, 128, 128), lambda j: (0, j, 0, 0))
    else:
        size = slots * hp * 128 + EXTRA
        out = jax.ShapeDtypeStruct((spread, size, 128), BF16)
        out_spec = pl.BlockSpec((1, size, 128), lambda j: (j, 0, 0))
    scratch = [pltpu.VMEM((slots, heads, rows), F32)]
    if not by_owner:
        scratch.append(pltpu.VMEM((heads, 128), F32))
    return pl.pallas_call(
        functools.partial(pieces_kernel, 128**-0.5, slots, by_owner),
        grid=(spread,),
        in_specs=[smem, smem, whole((heads, rows)), wide, wide],
        out_specs=[out_spec, whole((heads, rows)), whole((rows, heads))],
        out_shape=[
            out,
            jax.ShapeDtypeStruct((heads, rows), F32),
            jax.ShapeDtypeStruct((rows, heads), F32),
        ],
        scratch_shapes=scratch,
        compiler_params=pltpu.CompilerParams(vmem_limit_bytes=48 * 2**20),
        name="piece_states",
    )(doc_lengths, owner_ids, decay_rows, keys, values)


def head_column(ccol_ref, h):
    cols = ccol_ref[...]
    return jnp.sum(jnp.where(iota(cols.shape, 1) == h, cols, 0.0), axis=1, keepdims=True)


def blocks_kernel(scale, len_ref, q_ref, k_ref, v_ref, crow_ref, ccol_ref, out_ref, bias_ref):
    rows = q_ref.shape[0]
    count = len_ref.shape[0]
    step = pl.program_id(0)
    hb = q_ref.shape[1] // 128
    nblock = rows // BLK
    half = BLK // 2
    first = lax.axis_index("seq") * rows
    ends = read_ends(len_ref, count)

    @pl.when(step == 0)
    def _():
        for b in range(nblock):
            t_pos = first + b * BLK + iota((BLK, 1), 0)
            start = run_start(ends, t_pos)
            s_pos = first + b * BLK + iota((BLK, BLK), 1)
            keep = (s_pos <= t_pos) & (s_pos >= start)
            bias_ref[b * BLK : (b + 1) * BLK, :] = jnp.where(keep, math.log2(scale), NEG)

    for i in range(hb):
        h = step * hb + i
        col_all = head_column(ccol_ref, h)
        row_all = crow_ref[pl.ds(h, 1), :]
        lanes = slice(i * 128, (i + 1) * 128)
        carried = None
        for b in range(nblock):
            r0 = b * BLK
            key = k_ref[r0 : r0 + BLK, lanes]
            value = v_ref[r0 : r0 + BLK, lanes]
            if b > 0:
                before = first + r0 - 1
                reach = run_end(ends, before) - (first + r0)
                base = row_all[:, r0 - 1 : r0]
            for part in range(2):
                t0 = r0 + part * half
                width = (part + 1) * half
                query = q_ref[t0 : t0 + half, lanes]
                col = col_all[t0 : t0 + half]
                row = row_all[:, r0 : r0 + width]
                scores = dot(query, key[:width], ((1,), (1,)))
                decay = jnp.exp2((col - row) + bias_ref[t0 : t0 + half, :width])
                att = dot((scores * decay).astype(BF16), value[:width])
                if b > 0:
                    at = part * half + iota((half, 1), 0)
                    lead = jnp.exp2(jnp.where(at < reach, col - base, NEG))
                    att = att + lead * dot(query, carried_bf)
                out_ref[t0 : t0 + half, lanes] = att
            if b + 1 < nblock:
                last = first + r0 + BLK - 1
                since = run_start(ends, last) - (first + r0)
                row = row_all[:, r0 : r0 + BLK]
                total = row[:, BLK - 1 :]
                inside = iota((1, BLK), 1) >= since
                weight = jnp.exp2(jnp.where(inside, total - row, NEG) + math.log2(scale))
                weighted = (key.astype(F32).T * weight).astype(BF16)
                fresh = dot(weighted, value)
                if b > 0:
                    fresh = fresh + carried * jnp.exp2(jnp.where(BLK <= reach, total - base, NEG))
                carried = fresh
                carried_bf = carried.astype(BF16)


def block_attention(doc_lengths, queries, keys, values, crow, ccol):
    heads, rows = crow.shape
    hb = 2
    whole = lambda shape: pl.BlockSpec(shape, lambda j: (0,) * len(shape))
    wide = pl.BlockSpec((rows, hb * 128), lambda j: (0, j))
    return pl.pallas_call(
        functools.partial(blocks_kernel, 128**-0.5),
        grid=(heads // hb,),
        in_specs=[
            pl.BlockSpec(memory_space=pltpu.SMEM),
            wide,
            wide,
            wide,
            whole((heads, rows)),
            whole((rows, heads)),
        ],
        out_specs=wide,
        out_shape=jax.ShapeDtypeStruct((rows, heads * 128), F32),
        scratch_shapes=[pltpu.VMEM((rows, BLK), F32)],
        compiler_params=pltpu.CompilerParams(vmem_limit_bytes=48 * 2**20),
        cost_estimate=pl.CostEstimate(
            flops=heads * rows * BLK * 128 * 4, bytes_accessed=rows * heads * 128 * 10, transcendentals=heads * rows * BLK
        ),
        name="block_attention",
    )(doc_lengths, queries, keys, values, crow, ccol)


def scan_kernel(slots, rows, len_ref, own_ref, in_ref, enter_ref, final_ref, state_ref):
    spread, hp = enter_ref.shape[0], enter_ref.shape[1]
    count = len_ref.shape[0]
    ends = read_ends(len_ref, count)
    tail = slots * hp * 128

    def rate(e, i):
        extra = in_ref[e, tail:, :].astype(F32)
        return extra[i : i + 1, :] + extra[EXTRA // 2 + i : EXTRA // 2 + i + 1, :]

    def piece(e, s, i):
        return in_ref[e, pl.ds((s * hp + i) * 128, 128), :].astype(F32)

    for i in range(hp):
        state = jnp.zeros((128, 128), F32)
        for e in range(spread):
            state_ref[e, i] = state
            enter_ref[e, i] = state.astype(BF16)
            inner = jnp.int32(0)
            for d in range(count):
                inner = inner + ((ends[d] > e * rows) & (ends[d] < (e + 1) * rows)).astype(jnp.int32)
            passes = (inner == 0).astype(F32)
            state = state * (rate(e, i) * passes) + piece(e, 0, i)

    place, previous = jnp.int32(0), jnp.int32(-1)
    for d in range(count):
        device = (ends[d] - 1) // rows
        place = jnp.where(device == previous, place + 1, 0)
        previous = device
        at_end = ends[d] == (device + 1) * rows
        slot = jnp.where(at_end, 0, jnp.minimum(place, SIDE - 1) + 1)
        enters = (place == 0).astype(F32)
        for i in range(hp):
            start = pl.multiple_of((slot * hp + i) * 128, 128)
            local = in_ref[device, pl.ds(start, 128), :].astype(F32)
            state = local + state_ref[device, i] * (rate(device, i) * enters)
            final_ref[own_ref[d], i] = state.astype(BF16)


def scan_states(doc_lengths, owner_ids, parcels, slots, hp, rows):
    spread = parcels.shape[0]
    smem = pl.BlockSpec(memory_space=pltpu.SMEM)
    vmem = pl.BlockSpec(memory_space=pltpu.VMEM)
    shape = jax.ShapeDtypeStruct((spread, hp, 128, 128), BF16)
    return pl.pallas_call(
        functools.partial(scan_kernel, slots, rows),
        in_specs=[smem, smem, vmem],
        out_specs=[vmem, vmem],
        out_shape=[shape, shape],
        scratch_shapes=[pltpu.VMEM((spread, hp, 128, 128), F32)],
        compiler_params=pltpu.CompilerParams(vmem_limit_bytes=48 * 2**20),
        name="scan_states",
    )(doc_lengths, owner_ids, parcels)


def mix_kernel(len_ref, q_ref, enter_ref, local_ref, gate_ref, gain_ref, ccol_ref, out_ref):
    rows = q_ref.shape[0]
    step = pl.program_id(0)
    hb = q_ref.shape[1] // 128
    first = lax.axis_index("seq") * rows
    reach = run_end(read_ends(len_ref, len_ref.shape[0]), first - 1) - first
    at = iota((rows, 1), 0)
    for i in range(hb):
        lanes = slice(i * 128, (i + 1) * 128)
        col = head_column(ccol_ref, step * hb + i)
        lead = jnp.exp2(jnp.where(at < reach, col, NEG))
        att = local_ref[:, lanes] + lead * dot(q_ref[:, lanes], enter_ref[i])
        mean = jnp.mean(att * att, axis=1, keepdims=True)
        gate = 1.0 / (1.0 + jnp.exp(-gate_ref[:, lanes].astype(F32)))
        gain = gain_ref[:, lanes].astype(F32)
        out_ref[:, lanes] = (att * lax.rsqrt(mean + 1e-06) * gain * gate).astype(BF16)


def mix(doc_lengths, queries, entering, local, gate, gain, ccol):
    rows, heads = ccol.shape
    hb = 2
    wide = pl.BlockSpec((rows, hb * 128), lambda j: (0, j))
    return pl.pallas_call(
        mix_kernel,
        grid=(heads // hb,),
        in_specs=[
            pl.BlockSpec(memory_space=pltpu.SMEM),
            wide,
            pl.BlockSpec((hb, 128, 128), lambda j: (j, 0, 0)),
            wide,
            wide,
            pl.BlockSpec((1, hb * 128), lambda j: (0, j)),
            pl.BlockSpec((rows, heads), lambda j: (0, 0)),
        ],
        out_specs=wide,
        out_shape=jax.ShapeDtypeStruct((rows, heads * 128), BF16),
        compiler_params=pltpu.CompilerParams(vmem_limit_bytes=48 * 2**20),
        cost_estimate=pl.CostEstimate(
            flops=rows * heads * 128 * 256, bytes_accessed=rows * heads * 128 * 10, transcendentals=rows * heads * 128
        ),
        name="mix",
    )(doc_lengths, queries, entering, local, gate, gain.reshape(1, -1), ccol)


def swap(x):
    return lax.all_to_all(x, "seq", split_axis=0, concat_axis=0, tiled=True)


def crowded(doc_lengths, spread, rows, groups):
    count = doc_lengths.shape[0]
    index = jnp.arange(count, dtype=jnp.int32)
    ends = jnp.sum(jnp.where(index[None, :] <= index[:, None], doc_lengths[None, :], 0), axis=1)
    inner = (ends[None, :] // rows == jnp.arange(spread, dtype=jnp.int32)[:, None]) & (ends % rows != 0)[None, :]
    over = (jnp.max(jnp.sum(inner.astype(F32), axis=1)) > SIDE).astype(F32).reshape(1)
    seen = over
    for shift in range(1, groups):
        seen = seen + lax.ppermute(over, "groups", [(g, (g + shift) % groups) for g in range(groups)])
    return seen[0] > 0


def on_device(spread, groups, queries, keys, values, log_decay, gate, gain, doc_lengths, owner_ids):
    rows, heads = log_decay.shape
    hp = heads // spread
    slots = SIDE + 1
    decay_rows = log_decay.T
    over = crowded(doc_lengths, spread, rows, groups)
    parcels, crow, ccol = piece_states(doc_lengths, owner_ids, decay_rows, keys, values, spread, slots, False)
    parcels = swap(parcels)
    local = block_attention(doc_lengths, queries, keys, values, crow, ccol)
    entering, finals = scan_states(doc_lengths, owner_ids, parcels, slots, hp, rows)
    entering = swap(entering).reshape(heads, 128, 128)
    entering, finals = lax.optimization_barrier((entering, finals))
    owned = swap(finals).reshape(1, heads, 128, 128)
    mixed = mix(doc_lengths, queries, entering, local, gate, gain, ccol)

    def send_rest(owned):
        rest, _, _ = piece_states(doc_lengths, owner_ids, decay_rows, keys, values, spread, spread, True)
        rest = swap(rest)
        me = lax.axis_index("seq")
        index = jnp.arange(owner_ids.shape[0], dtype=jnp.int32)
        ends = jnp.cumsum(doc_lengths)
        doc = jnp.sum(jnp.where(owner_ids == me, index, 0))
        source = (ends - 1) // rows
        mine = source[doc]
        ahead = jnp.sum(((source == mine) & (index < doc)).astype(jnp.int32))
        late = (ahead >= SIDE) & (ends[doc] % rows != 0)
        return jnp.where(late, lax.dynamic_index_in_dim(rest, mine, 0, True), owned)

    owned = lax.cond(over, send_rest, lambda owned: owned, owned)
    return mixed, owned


def solution(mesh):
    placed = (
        P(("groups", "seq"), "tp"),
        P(("groups", "seq"), "tp"),
        P(("groups", "seq"), "tp"),
        P(("groups", "seq"), "tp"),
        P(("groups", "seq"), "tp"),
        P("tp"),
        P("groups"),
        P("groups"),
    )
    return jax.shard_map(
        functools.partial(on_device, mesh.shape["seq"], mesh.shape["groups"]),
        mesh=mesh,
        in_specs=placed,
        out_specs=(P(("groups", "seq"), "tp"), P(("groups", "seq"), "tp", None, None)),
        check_vma=False,
    )
```

time: 397 us -> 130 us (0.33)
  waiting for transfers between devices: 147 us -> 13.6 us
  local copies, waits for them, and re-layouts: 71.2 us -> 3.01 us
  matrix products: 53.4 us -> 0 us
  Pallas kernels: 0 us -> 43.3 us
  blocking collectives: 23.7 us -> 56.9 us
  other arithmetic: 30.1 us -> 0.86 us
  loops' own time: 26.1 us -> 0.01 us
  starting transfers between devices: 24.9 us -> 9.98 us
  between operations: 16.3 us -> 1.96 us
    all_gather x1 -> x0, waiting for transfers between devices: 93.5 us -> none  [entering(): gathered = jax.tree.map(lambda a: lax.all_gather(a, axis), part)]
    all_to_all x0 -> x1, blocking collectives: none -> 56.9 us  [swap(): return lax.all_to_all(x, 'seq', split_axis=0, concat_axis=0, tiled=True)]
    dot_general x7 -> x0, matrix products: 53.4 us -> none  [the longest x2 23.4 us: local_intra(): jnp.einsum('hij,jhd->ihd', weights, value_part, preferred_element_type=jn...]
    pallas_call x0 -> x4, Pallas kernels: none -> 43.3 us  [the longest x1 18.7 us: block_attention(): pl.pallas_call(functools.partial(blocks_kernel, 128 ** (-0.5)), grid=(hea...]
    all_to_all x1 -> x2, waiting for transfers between devices: 53.6 us -> 13.6 us  [swap(): return lax.all_to_all(x, 'seq', split_axis=0, concat_axis=0, tiled=True)]
    another operation x11 -> x1, loops' own time: 26.1 us -> 0.01 us  [on_device(): owned = lax.cond(over, send_rest, lambda owned: owned, owned)]
    unnamed x1 -> x0, blocking collectives: 23.7 us -> none
    all_to_all x1 -> x2, starting transfers between devices: 24.9 us -> 7.11 us  [swap(): return lax.all_to_all(x, 'seq', split_axis=0, concat_axis=0, tiled=True)]
  transfers between devices with their start and end apart: 2 -> 3, of which waited for: 2 -> 1; matrix products, arithmetic and copies ran while one was open for 12% -> 1% of each run, Pallas kernels for 0% -> 23%
where the time goes in v1:
time: 130 us
  blocking collectives  56.9 us (44%)
  Pallas kernels  43.3 us (33%)
  waiting for transfers between devices  13.6 us (10%)
  starting transfers between devices  9.98 us (8%)
  local copies, waits for them, and re-layouts  3.01 us (2%)
  between operations  1.96 us (2%)
    all_to_all x1, blocking collectives, swap(): return lax.all_to_all(x, 'seq', split_axis=0, concat_axis=0, tiled=True)  56.9 us
    pallas_call x1, Pallas kernels, block_attention(): pl.pallas_call(functools.partial(blocks_kernel, 128 ** (-0.5)), grid=(hea...  18.7 us
    all_to_all x2, waiting for transfers between devices, swap(): return lax.all_to_all(x, 'seq', split_axis=0, concat_axis=0, tiled=True)  13.6 us
    pallas_call x1, Pallas kernels, mix(): pl.pallas_call(mix_kernel, grid=(heads // hb,), in_specs=[pl.BlockSpec(me...  11.7 us
    pallas_call x1, Pallas kernels, piece_states(): pl.pallas_call(functools.partial(pieces_kernel, 128 ** (-0.5), slots, by_...  11.1 us
    all_to_all x2, starting transfers between devices, swap(): return lax.all_to_all(x, 'seq', split_axis=0, concat_axis=0, tiled=True)  7.11 us
    unnamed x13, local copies, waits for them, and re-layouts  3.01 us
    ppermute x1, starting transfers between devices, crowded(): lax.ppermute(over, 'groups', [(g, (g + shift) % groups) for g in range(gr...  2.87 us
  transfers between devices with their start and end apart: 3, of which 1 were waited for; matrix products, arithmetic and copies ran while one was open for 1% of the time, Pallas kernels for 23%

profile of v1, /device:TPU:0, one launch (start us, length us, event | category | flops | bytes accessed | tf_op | source)
XLA Modules:
  0.0 129.7 jit_solution(1862202491995937655)
XLA Ops:
  0.6 11.1 %piece_states.3 = (bf16[8,1040,128]{2,1,0:T(8,128)(2,1)S(1)}, f32[16,1024]{1,0:T(8,128)S(1)}, f32[1024,16]{1,0:T(8,128)S(1)}) custom-call(s32[8]{0:T(128)} %len_ref.7, s32[8]{0:T(128)} %own_ref.3, f32[16,1024]{1,0:T(8,128)} %bitcast.21, bf16[1024,2048]{1,0:T(8,128)(2,1)} %k_ref.3, bf16[1024,2048]{1,0:T(8,128)(2,1)} %v_ref.3), custom_call_target="tpu_custom_call" | custom-call | tf_op jit(solution)/shard_map/piece_states/pallas_call | solution.py:159
  11.8 0.0 copy-start.4
  11.8 0.0 copy-start.5
  11.8 0.0 copy-start.6
  11.8 56.9 %all_to_all.19.in_ref = bf16[8,1040,128]{2,1,0:T(8,128)(2,1)S(1)} all-to-all(bf16[8,1040,128]{2,1,0:T(8,128)(2,1)S(1)} %get-tuple-element.32), channel_id=1, replica_groups=mesh['groups'=2,'seq'=8,'tp'=2] {'seq'}, dimensions={0} | all-to-all | bytes 4259840 | tf_op jit(solution)/shard_map/all_to_all | solution.py:369
  68.7 0.0 copy-done.4
  68.7 0.0 copy-done.5
  68.7 1.8 %scan_states.1 = (bf16[8,2,128,128]{3,2,1,0:T(8,128)(2,1)}, bf16[8,2,128,128]{3,2,1,0:T(8,128)(2,1)}) custom-call(s32[8]{0:T(128)S(1)} %copy-done.4, s32[8]{0:T(128)S(1)} %copy-done.5, bf16[8,1040,128]{2,1,0:T(8,128)(2,1)S(1)} %all_to_all.19.in_ref), custom_call_target="tpu_custom_call" | custom-call | tf_op jit(solution)/shard_map/scan_states/pallas_call | solution.py:313
  70.5 3.5 %all-to-all-start.2 = ((bf16[8,2,128,128]{3,2,1,0:T(8,128)(2,1)}), bf16[8,2,128,128]{3,2,1,0:T(8,128)(2,1)S(1)}, u32[]{:S(2)}, u32[]{:S(2)}) async-start(bf16[8,2,128,128]{3,2,1,0:T(8,128)(2,1)} %get-tuple-element.33), calls=%async_computation.2 | async-start | bytes 1048576 | tf_op jit(solution)/shard_map/all_to_all | solution.py:369
  74.0 0.1 select_reduce_fusion
  74.1 13.6 %all-to-all-done.2 = bf16[8,2,128,128]{3,2,1,0:T(8,128)(2,1)S(1)} async-done(((bf16[8,2,128,128]{3,2,1,0:T(8,128)(2,1)}), bf16[8,2,128,128]{3,2,1,0:T(8,128)(2,1)S(1)}, u32[]{:S(2)}, u32[]{:S(2)}) %all-to-all-start.2) | async-done | bytes 524320 | tf_op jit(solution)/shard_map/all_to_all | solution.py:369
  87.8 3.6 %all-to-all-start.3 = ((bf16[8,2,128,128]{3,2,1,0:T(8,128)(2,1)}), bf16[8,2,128,128]{3,2,1,0:T(8,128)(2,1)S(1)}, u32[]{:S(2)}, u32[]{:S(2)}) async-start(bf16[8,2,128,128]{3,2,1,0:T(8,128)(2,1)} %get-tuple-element.38), calls=%async_computation.3 | async-start | bytes 1048576 | tf_op jit(solution)/shard_map/all_to_all | solution.py:369
  91.4 0.1 convert_reduce_fusion
  91.5 0.6 reduce_max.9
  92.8 2.9 %collective-permute-start = (f32[1]{0:T(128)}, f32[1]{0:T(128)}, u32[]{:S(2)}, u32[]{:S(2)}) collective-permute-start(f32[1]{0:T(128)} %bitcast.6), channel_id=1, source_target_pairs={{0,16},{16,0},{1,17},{17,1},{2,18},{18,2},{3,19},{19,3},{4,20},{20... | collective-permute-start | bytes 20 | tf_op jit(solution)/shard_map/ppermute | solution.py:380
  95.7 0.0 copy-done.6
  95.7 0.0 copy-start
  95.7 2.2 %copy-done = bf16[1024,2048]{1,0:T(8,128)(2,1)S(1)} copy-done((bf16[1024,2048]{1,0:T(8,128)(2,1)S(1)}, bf16[1024,2048]{1,0:T(8,128)(2,1)}, u32[]{:S(2)}) %copy-start) | copy-done | bytes 4194328
  97.9 0.0 copy-start.1
  97.9 18.7 %block_attention.1.local_ref = f32[1024,2048]{1,0:T(8,128)} custom-call(s32[8]{0:T(128)S(1)} %copy-done.4, bf16[1024,2048]{1,0:T(8,128)(2,1)S(1)} %copy-done, bf16[1024,2048]{1,0:T(8,128)(2,1)} %k_ref.3, bf16[1024,2048]{1,0:T(8,128)(2,1)} %v_ref.3, f32[16,1024]{1,0:T(8,128)S(1)} %get-tuple-element.36.crow_ref, f32[1024,16]{1,0:T(8,128)S(1)} %get-tuple-element.37.ccol_ref), custom_call_target="tpu_custom_call" | custom-call | flops 4294967296 | bytes 20971520 | tf_op jit(solution)/shard_map/block_attention/pallas_call | solution.py:247
  116.6 0.0 collective-permute-done
  117.2 0.0 copy-done.1
  117.2 0.0 copy-start.3
  117.2 11.7 %mix.1 = bf16[1024,2048]{1,0:T(8,128)(2,1)} custom-call(s32[8]{0:T(128)S(1)} %copy-done.4, bf16[1024,2048]{1,0:T(8,128)(2,1)S(1)} %copy-done.1, bf16[16,128,128]{2,1,0:T(8,128)(2,1)S(1)} %bitcast.18, f32[1024,2048]{1,0:T(8,128)} %block_attention.1.local_ref, bf16[1024,2048]{1,0:T(8,128)(2,1)} %gate_ref.1, bf16[1,2048]{1,0:T(2,128)(2,1)S(1)} %reshape.85.gain_ref, ...), custom_call_target="tpu_custom_call" | custom-call | flops 536870912 | bytes 20971520 | tf_op jit(solution)/shard_map/mix/pallas_call | solution.py:346
  128.9 0.0 all-to-all-done.3
  128.9 0.0 copy-done.3
  128.9 0.8 copy.13
  (4 shorter events, 0.0 us)
Async XLA Ops:
  11.8 56.9 %copy-start.4 = (s32[8]{0:T(128)S(1)}, s32[8]{0:T(128)}, u32[]{:S(2)}) copy-start(s32[8]{0:T(128)} %len_ref.7) | copy-start | bytes 100
  11.8 56.9 %copy-start.5 = (s32[8]{0:T(128)S(1)}, s32[8]{0:T(128)}, u32[]{:S(2)}) copy-start(s32[8]{0:T(128)} %own_ref.3) | copy-start | bytes 100
  11.8 83.9 %copy-start.6 = (bf16[2048]{0:T(1024)(128)(2,1)S(1)}, bf16[2048]{0:T(1024)(128)(2,1)}, u32[]{:S(2)}) copy-start(bf16[2048]{0:T(1024)(128)(2,1)} %param.15) | copy-start | bytes 12292
  70.5 17.3 %all-to-all-start.2 = ((bf16[8,2,128,128]{3,2,1,0:T(8,128)(2,1)}), bf16[8,2,128,128]{3,2,1,0:T(8,128)(2,1)S(1)}, u32[]{:S(2)}, u32[]{:S(2)}) async-start(bf16[8,2,128,128]{3,2,1,0:T(8,128)(2,1)} %get-tuple-element.33), calls=%async_computation.2 | async-start | bytes 1048576 | tf_op jit(solution)/shard_map/all_to_all | solution.py:369
  87.8 41.1 %all-to-all-start.3 = ((bf16[8,2,128,128]{3,2,1,0:T(8,128)(2,1)}), bf16[8,2,128,128]{3,2,1,0:T(8,128)(2,1)S(1)}, u32[]{:S(2)}, u32[]{:S(2)}) async-start(bf16[8,2,128,128]{3,2,1,0:T(8,128)(2,1)} %get-tuple-element.38), calls=%async_computation.3 | async-start | bytes 1048576 | tf_op jit(solution)/shard_map/all_to_all | solution.py:369
  92.8 23.8 %collective-permute-start = (f32[1]{0:T(128)}, f32[1]{0:T(128)}, u32[]{:S(2)}, u32[]{:S(2)}) collective-permute-start(f32[1]{0:T(128)} %bitcast.6), channel_id=1, source_target_pairs={{0,16},{16,0},{1,17},{17,1},{2,18},{18,2},{3,19},{19,3},{4,20},{20... | collective-permute-start | bytes 20 | tf_op jit(solution)/shard_map/ppermute | solution.py:380
  95.7 2.2 %copy-start = (bf16[1024,2048]{1,0:T(8,128)(2,1)S(1)}, bf16[1024,2048]{1,0:T(8,128)(2,1)}, u32[]{:S(2)}) copy-start(bf16[1024,2048]{1,0:T(8,128)(2,1)} %q_ref.3) | copy-start | bytes 12582916
  97.9 19.3 %copy-start.1 = (bf16[1024,2048]{1,0:T(8,128)(2,1)S(1)}, bf16[1024,2048]{1,0:T(8,128)(2,1)}, u32[]{:S(2)}) copy-start(bf16[1024,2048]{1,0:T(8,128)(2,1)} %q_ref.3) | copy-start | bytes 12582916
  117.2 11.7 %copy-start.3 = (f32[1024,16]{0,1:T(8,128)S(1)}, f32[1024,16]{0,1:T(8,128)}, u32[]{:S(2)}) copy-start(f32[1024,16]{0,1:T(8,128)} %param.13) | copy-start | bytes 196612

commit v2 on v1

v2 whole, which is shorter than its diff:
```python
import functools
import math

import jax
import jax.numpy as jnp
from jax import lax
from jax.experimental import pallas as pl
from jax.experimental.pallas import tpu as pltpu
from jax.sharding import PartitionSpec as P

BLK = 512
SIDE = 3
EXTRA = 16
NEG = -1e30
LOG2E = math.log2(math.e)
SCALE = 128**-0.5
F32, BF16 = jnp.float32, jnp.bfloat16
SMEM = pl.BlockSpec(memory_space=pltpu.SMEM)
VMEM = pl.BlockSpec(memory_space=pltpu.VMEM)
LIMIT = pltpu.CompilerParams(vmem_limit_bytes=48 * 2**20)


def dot(a, b, contract=((1,), (0,))):
    return lax.dot_general(a, b, (contract, ((), ())), preferred_element_type=F32)


def iota(shape, dim):
    return lax.broadcasted_iota(jnp.int32, shape, dim)


def read_ends(len_ref, count):
    ends, total = [], jnp.int32(0)
    for d in range(count):
        total = total + len_ref[d]
        ends.append(total)
    return ends


def run_end(ends, pos):
    best = ends[-1]
    for e in reversed(ends[:-1]):
        best = jnp.where(e > pos, e, best)
    return best


def run_start(ends, pos):
    best = jnp.zeros_like(pos)
    for e in ends[:-1]:
        best = jnp.where(e <= pos, e, best)
    return best


def split3(x):
    hi = x.astype(BF16)
    rest = x - hi.astype(F32)
    mid = rest.astype(BF16)
    return hi, mid, (rest - mid.astype(F32)).astype(BF16)


def cum_rows(ld_ref, crow_ref):
    heads, rows = ld_ref.shape
    upper = (iota((BLK, BLK), 0) <= iota((BLK, BLK), 1)).astype(F32).astype(BF16)
    base = jnp.zeros((heads, 1), F32)
    for b in range(rows // BLK):
        part = ld_ref[:, b * BLK : (b + 1) * BLK] * LOG2E
        row = jnp.zeros((heads, BLK), F32)
        for piece in reversed(split3(part)):
            row = row + dot(piece, upper)
        row = row + base
        crow_ref[:, b * BLK : (b + 1) * BLK] = row
        base = row[:, BLK - 1 :]


def value_at(cum, at, index):
    return jnp.sum(jnp.where(at == index, cum, 0.0), axis=1, keepdims=True)


def span_weights(cum, at, low, high):
    inside = (at >= low) & (at <= high)
    return jnp.exp2(jnp.where(inside, value_at(cum, at, high) - cum, NEG) + math.log2(SCALE))


def last_kernel(len_ref, ld_ref, k_ref, v_ref, out_ref, crow_ref, w_ref, first_ref):
    heads, rows = ld_ref.shape
    step = pl.program_id(0)
    hp = k_ref.shape[1] // 128

    @pl.when(step == 0)
    def _():
        cum_rows(ld_ref, crow_ref)
        first = lax.axis_index("seq") * rows
        ends = read_ends(len_ref, len_ref.shape[0])
        at = iota((heads, rows), 1)
        cum = crow_ref[...]
        low = jnp.maximum(run_start(ends, first + rows - 1) - first, 0)
        w_ref[...] = span_weights(cum, at, low, rows - 1)
        stop = jnp.minimum(run_end(ends, first) - 1 - first, rows - 1)
        goes_on = (run_start(ends, first) < first).astype(F32)
        first_ref[...] = jnp.broadcast_to(jnp.exp2(value_at(cum, at, stop)) * goes_on, (heads, 128))

    for i in range(hp):
        lanes = slice(i * 128, (i + 1) * 128)
        flipped = k_ref[:, lanes].T.astype(F32)
        weighted = (flipped * w_ref[pl.ds(step * hp + i, 1), :]).astype(BF16)
        out_ref[0, lanes, :] = dot(weighted, v_ref[:, lanes]).astype(BF16)
    rate = first_ref[pl.ds(step * hp, hp), :]
    high = rate.astype(BF16).astype(F32)
    pad = jnp.zeros((EXTRA - 2 * hp, 128), F32)
    out_ref[0, hp * 128 :, :] = jnp.concatenate([high, rate - high, pad], axis=0).astype(BF16)


def whole(shape):
    return pl.BlockSpec(shape, lambda j: (0,) * len(shape))


def last_pieces(doc_lengths, decay_rows, keys, values, members):
    heads, rows = decay_rows.shape
    hp = heads // members
    wide = pl.BlockSpec((rows, hp * 128), lambda j: (0, j))
    size = hp * 128 + EXTRA
    return pl.pallas_call(
        last_kernel,
        grid=(members,),
        in_specs=[SMEM, whole((heads, rows)), wide, wide],
        out_specs=[pl.BlockSpec((1, size, 128), lambda j: (j, 0, 0)), whole((heads, rows))],
        out_shape=[
            jax.ShapeDtypeStruct((members, size, 128), BF16),
            jax.ShapeDtypeStruct((heads, rows), F32),
        ],
        scratch_shapes=[pltpu.VMEM((heads, rows), F32), pltpu.VMEM((heads, 128), F32)],
        compiler_params=LIMIT,
        cost_estimate=pl.CostEstimate(
            flops=heads * rows * 128 * 256, bytes_accessed=rows * heads * 128 * 4, transcendentals=heads * rows
        ),
        name="last_pieces",
    )(doc_lengths, decay_rows, keys, values)


def side_kernel(slots, by_owner, len_ref, own_ref, ld_ref, crow_ref, k_ref, v_ref, out_ref, ccol_ref, w_ref):
    heads, rows = crow_ref.shape
    step = pl.program_id(0)
    hp = k_ref.shape[1] // 128

    @pl.when(step == 0)
    def _():
        lower = (iota((BLK, BLK), 0) >= iota((BLK, BLK), 1)).astype(F32).astype(BF16)
        base = jnp.zeros((1, heads), F32)
        for b in range(rows // BLK):
            part = ld_ref[:, b * BLK : (b + 1) * BLK] * LOG2E
            col = jnp.zeros((BLK, heads), F32)
            for piece in reversed(split3(part)):
                col = col + dot(lower, piece, ((1,), (1,)))
            col = col + base
            ccol_ref[b * BLK : (b + 1) * BLK, :] = col
            base = col[BLK - 1 :, :]
        first = lax.axis_index("seq") * rows
        last = first + rows - 1
        ends = read_ends(len_ref, len_ref.shape[0])
        starts = [jnp.int32(0)] + ends[:-1]
        lows = [jnp.int32(0)] * slots
        highs = [jnp.int32(-1)] * slots
        place = jnp.int32(0)
        for d in range(len(ends)):
            here = (ends[d] > first) & (ends[d] <= last)
            low = jnp.maximum(starts[d] - first, 0)
            for s in range(slots):
                mine = here & ((place >= SIDE) & (own_ref[d] == s) if by_owner else (place == s))
                lows[s] = jnp.where(mine, low, lows[s])
                highs[s] = jnp.where(mine, ends[d] - 1 - first, highs[s])
            place = place + here.astype(jnp.int32)
        at = iota((heads, rows), 1)
        cum = crow_ref[...]
        for s in range(slots):
            w_ref[s] = span_weights(cum, at, lows[s], highs[s])

    for i in range(hp):
        lanes = slice(i * 128, (i + 1) * 128)
        flipped = k_ref[:, lanes].T.astype(F32)
        for s in range(slots):
            weighted = (flipped * w_ref[s, pl.ds(step * hp + i, 1), :]).astype(BF16)
            state = dot(weighted, v_ref[:, lanes]).astype(BF16)
            if by_owner:
                out_ref[s, i] = state
            else:
                at = (s * hp + i) * 128
                out_ref[0, at : at + 128, :] = state


def side_pieces(doc_lengths, owner_ids, decay_rows, crow, keys, values, members, slots, by_owner):
    heads, rows = crow.shape
    hp = heads // members
    wide = pl.BlockSpec((rows, hp * 128), lambda j: (0, j))
    if by_owner:
        out = jax.ShapeDtypeStruct((slots, heads, 128, 128), BF16)
        out_spec = pl.BlockSpec((slots, hp, 128, 128), lambda j: (0, j, 0, 0))
    else:
        out = jax.ShapeDtypeStruct((members, slots * hp * 128, 128), BF16)
        out_spec = pl.BlockSpec((1, slots * hp * 128, 128), lambda j: (j, 0, 0))
    return pl.pallas_call(
        functools.partial(side_kernel, slots, by_owner),
        grid=(members,),
        in_specs=[SMEM, SMEM, whole((heads, rows)), whole((heads, rows)), wide, wide],
        out_specs=[out_spec, whole((rows, heads))],
        out_shape=[out, jax.ShapeDtypeStruct((rows, heads), F32)],
        scratch_shapes=[pltpu.VMEM((slots, heads, rows), F32)],
        compiler_params=LIMIT,
        cost_estimate=pl.CostEstimate(
            flops=slots * heads * rows * 128 * 256, bytes_accessed=rows * heads * 128 * 4, transcendentals=heads * rows
        ),
        name="side_pieces",
    )(doc_lengths, owner_ids, decay_rows, crow, keys, values)


def head_column(ccol_ref, h):
    cols = ccol_ref[...]
    return jnp.sum(jnp.where(iota(cols.shape, 1) == h, cols, 0.0), axis=1, keepdims=True)


def blocks_kernel(len_ref, q_ref, k_ref, v_ref, crow_ref, ccol_ref, out_ref, bias_ref):
    rows = q_ref.shape[0]
    count = len_ref.shape[0]
    step = pl.program_id(0)
    hb = q_ref.shape[1] // 128
    nblock = rows // BLK
    half = BLK // 2
    first = lax.axis_index("seq") * rows
    ends = read_ends(len_ref, count)

    @pl.when(step == 0)
    def _():
        for b in range(nblock):
            t_pos = first + b * BLK + iota((BLK, 1), 0)
            start = run_start(ends, t_pos)
            s_pos = first + b * BLK + iota((BLK, BLK), 1)
            keep = (s_pos <= t_pos) & (s_pos >= start)
            bias_ref[b * BLK : (b + 1) * BLK, :] = jnp.where(keep, math.log2(SCALE), NEG)

    for i in range(hb):
        h = step * hb + i
        col_all = head_column(ccol_ref, h)
        row_all = crow_ref[pl.ds(h, 1), :]
        lanes = slice(i * 128, (i + 1) * 128)
        carried = None
        for b in range(nblock):
            r0 = b * BLK
            key = k_ref[r0 : r0 + BLK, lanes]
            value = v_ref[r0 : r0 + BLK, lanes]
            if b > 0:
                before = first + r0 - 1
                reach = run_end(ends, before) - (first + r0)
                base = row_all[:, r0 - 1 : r0]
            for part in range(2):
                t0 = r0 + part * half
                width = (part + 1) * half
                query = q_ref[t0 : t0 + half, lanes]
                col = col_all[t0 : t0 + half]
                row = row_all[:, r0 : r0 + width]
                scores = dot(query, key[:width], ((1,), (1,)))
                decay = jnp.exp2((col - row) + bias_ref[t0 : t0 + half, :width])
                att = dot((scores * decay).astype(BF16), value[:width])
                if b > 0:
                    at = part * half + iota((half, 1), 0)
                    lead = jnp.exp2(jnp.where(at < reach, col - base, NEG))
                    att = att + lead * dot(query, carried_bf)
                out_ref[t0 : t0 + half, lanes] = att
            if b + 1 < nblock:
                last = first + r0 + BLK - 1
                since = run_start(ends, last) - (first + r0)
                row = row_all[:, r0 : r0 + BLK]
                total = row[:, BLK - 1 :]
                inside = iota((1, BLK), 1) >= since
                weight = jnp.exp2(jnp.where(inside, total - row, NEG) + math.log2(SCALE))
                weighted = (key.astype(F32).T * weight).astype(BF16)
                fresh = dot(weighted, value)
                if b > 0:
                    fresh = fresh + carried * jnp.exp2(jnp.where(BLK <= reach, total - base, NEG))
                carried = fresh
                carried_bf = carried.astype(BF16)


def block_attention(doc_lengths, queries, keys, values, crow, ccol):
    heads, rows = crow.shape
    hb = 2
    wide = pl.BlockSpec((rows, hb * 128), lambda j: (0, j))
    return pl.pallas_call(
        blocks_kernel,
        grid=(heads // hb,),
        in_specs=[
            SMEM,
            wide,
            wide,
            wide,
            whole((heads, rows)),
            whole((rows, heads)),
        ],
        out_specs=wide,
        out_shape=jax.ShapeDtypeStruct((rows, heads * 128), F32),
        scratch_shapes=[pltpu.VMEM((rows, BLK), F32)],
        compiler_params=LIMIT,
        cost_estimate=pl.CostEstimate(
            flops=heads * rows * BLK * 128 * 4, bytes_accessed=rows * heads * 128 * 10, transcendentals=heads * rows * BLK
        ),
        name="block_attention",
    )(doc_lengths, queries, keys, values, crow, ccol)


def decay_of(last_ref, e, i, hp):
    extra = last_ref[e, hp * 128 :, :].astype(F32)
    return extra[i : i + 1, :] + extra[hp + i : hp + i + 1, :]


def scan_quad(rows, len_ref, last_ref, state, i, hp, note):
    members = last_ref.shape[0]
    ends = read_ends(len_ref, len_ref.shape[0])
    base = lax.axis_index("seq") // members * members
    for e in range(members):
        note(e, state)
        low = (base + e) * rows
        inner = jnp.int32(0)
        for end in ends:
            inner = inner + ((end > low) & (end < low + rows)).astype(jnp.int32)
        passes = (inner == 0).astype(F32)
        piece = last_ref[e, i * 128 : (i + 1) * 128, :].astype(F32)
        state = state * (decay_of(last_ref, e, i, hp) * passes) + piece
    return state


def leave_kernel(rows, len_ref, last_ref, in_ref, out_ref):
    hp = in_ref.shape[0]
    for i in range(hp):
        state = scan_quad(rows, len_ref, last_ref, in_ref[i].astype(F32), i, hp, lambda e, x: None)
        out_ref[i] = state.astype(BF16)


def leave_quad(doc_lengths, last, coming, rows):
    return pl.pallas_call(
        functools.partial(leave_kernel, rows),
        in_specs=[SMEM, VMEM, VMEM],
        out_specs=VMEM,
        out_shape=jax.ShapeDtypeStruct(coming.shape, BF16),
        compiler_params=LIMIT,
        name="leave_quad",
    )(doc_lengths, last, coming)


def enter_kernel(rows, len_ref, last_ref, in_ref, out_ref):
    hp = in_ref.shape[0]

    def note(i, e, state):
        out_ref[e, i] = state.astype(BF16)

    for i in range(hp):
        scan_quad(rows, len_ref, last_ref, in_ref[i].astype(F32), i, hp, functools.partial(note, i))


def enter_states(doc_lengths, last, coming, rows):
    return pl.pallas_call(
        functools.partial(enter_kernel, rows),
        in_specs=[SMEM, VMEM, VMEM],
        out_specs=VMEM,
        out_shape=jax.ShapeDtypeStruct((last.shape[0],) + coming.shape, BF16),
        compiler_params=LIMIT,
        name="enter_states",
    )(doc_lengths, last, coming)


def final_kernel(rows, len_ref, own_ref, last_ref, side_ref, in_ref, out_ref, state_ref):
    hp = in_ref.shape[0]
    members = last_ref.shape[0]
    ends = read_ends(len_ref, len_ref.shape[0])
    base = lax.axis_index("seq") // members * members

    def note(i, e, state):
        state_ref[e, i] = state

    for i in range(hp):
        scan_quad(rows, len_ref, last_ref, in_ref[i].astype(F32), i, hp, functools.partial(note, i))
    out_ref[...] = jnp.zeros_like(out_ref)
    place, previous = jnp.int32(0), jnp.int32(-1)
    for d in range(len(ends)):
        device = (ends[d] - 1) // rows
        place = jnp.where(device == previous, place + 1, 0)
        previous = device
        at_end = ends[d] == (device + 1) * rows
        enters = (place == 0).astype(F32)
        mine = device // members * members == base
        e = device - base

        def put(i, local):
            state = local.astype(F32) + state_ref[e, i] * (decay_of(last_ref, e, i, hp) * enters)
            out_ref[own_ref[d], i] = state.astype(BF16)

        @pl.when(mine & at_end)
        def _():
            for i in range(hp):
                put(i, last_ref[e, i * 128 : (i + 1) * 128, :])

        @pl.when(mine & jnp.logical_not(at_end))
        def _():
            for i in range(hp):
                row = pl.multiple_of((jnp.minimum(place, SIDE - 1) * hp + i) * 128, 128)
                put(i, side_ref[e, pl.ds(row, 128), :])


def final_states(doc_lengths, owner_ids, last, side, coming, rows, spread):
    return pl.pallas_call(
        functools.partial(final_kernel, rows),
        in_specs=[SMEM, SMEM, VMEM, VMEM, VMEM],
        out_specs=VMEM,
        out_shape=jax.ShapeDtypeStruct((spread,) + coming.shape, BF16),
        scratch_shapes=[pltpu.VMEM((last.shape[0],) + coming.shape, F32)],
        compiler_params=LIMIT,
        name="final_states",
    )(doc_lengths, owner_ids, last, side, coming)


def mix_kernel(len_ref, q_ref, enter_ref, local_ref, gate_ref, gain_ref, ccol_ref, out_ref):
    rows = q_ref.shape[0]
    step = pl.program_id(0)
    hb = q_ref.shape[1] // 128
    first = lax.axis_index("seq") * rows
    reach = run_end(read_ends(len_ref, len_ref.shape[0]), first - 1) - first
    at = iota((rows, 1), 0)
    for i in range(hb):
        lanes = slice(i * 128, (i + 1) * 128)
        col = head_column(ccol_ref, step * hb + i)
        lead = jnp.exp2(jnp.where(at < reach, col, NEG))
        att = local_ref[:, lanes] + lead * dot(q_ref[:, lanes], enter_ref[i])
        mean = jnp.mean(att * att, axis=1, keepdims=True)
        gate = 1.0 / (1.0 + jnp.exp(-gate_ref[:, lanes].astype(F32)))
        gain = gain_ref[:, lanes].astype(F32)
        out_ref[:, lanes] = (att * lax.rsqrt(mean + 1e-06) * gain * gate).astype(BF16)


def mix(doc_lengths, queries, entering, local, gate, gain, ccol):
    rows, heads = ccol.shape
    hb = 2
    wide = pl.BlockSpec((rows, hb * 128), lambda j: (0, j))
    return pl.pallas_call(
        mix_kernel,
        grid=(heads // hb,),
        in_specs=[
            SMEM,
            wide,
            pl.BlockSpec((hb, 128, 128), lambda j: (j, 0, 0)),
            wide,
            wide,
            pl.BlockSpec((1, hb * 128), lambda j: (0, j)),
            pl.BlockSpec((rows, heads), lambda j: (0, 0)),
        ],
        out_specs=wide,
        out_shape=jax.ShapeDtypeStruct((rows, heads * 128), BF16),
        compiler_params=LIMIT,
        cost_estimate=pl.CostEstimate(
            flops=rows * heads * 128 * 256, bytes_accessed=rows * heads * 128 * 10, transcendentals=rows * heads * 128
        ),
        name="mix",
    )(doc_lengths, queries, entering, local, gate, gain.reshape(1, -1), ccol)


def swap(x, groups=None):
    return lax.all_to_all(x, "seq", split_axis=0, concat_axis=0, axis_index_groups=groups, tiled=True)


def crowded(doc_lengths, spread, rows, groups):
    count = doc_lengths.shape[0]
    index = jnp.arange(count, dtype=jnp.int32)
    ends = jnp.sum(jnp.where(index[None, :] <= index[:, None], doc_lengths[None, :], 0), axis=1)
    inner = (ends[None, :] // rows == jnp.arange(spread, dtype=jnp.int32)[:, None]) & (ends % rows != 0)[None, :]
    over = (jnp.max(jnp.sum(inner.astype(F32), axis=1)) > SIDE).astype(F32).reshape(1)
    seen = over
    for shift in range(1, groups):
        seen = seen + lax.ppermute(over, "groups", [(g, (g + shift) % groups) for g in range(groups)])
    return seen[0] > 0


def own_final(doc_lengths, owner_ids, rows):
    index = jnp.arange(owner_ids.shape[0], dtype=jnp.int32)
    ends = jnp.sum(jnp.where(index[None, :] <= index[:, None], doc_lengths[None, :], 0), axis=1)
    mine = owner_ids == lax.axis_index("seq")
    source = (ends - 1) // rows
    device = jnp.sum(jnp.where(mine, source, 0))
    doc = jnp.sum(jnp.where(mine, index, 0))
    ahead = jnp.sum(((source == device) & (index < doc)).astype(jnp.int32))
    inner = jnp.sum(jnp.where(mine, ends, 0)) != (device + 1) * rows
    return device, (ahead >= SIDE) & inner


def on_device(spread, groups, queries, keys, values, log_decay, gate, gain, doc_lengths, owner_ids):
    rows, heads = log_decay.shape
    members = 4
    quads = spread // members
    hp = heads // members
    near = [[q * members + m for m in range(members)] for q in range(quads)]
    onward = [(s, s + members) for s in range(spread - members)]
    decay_rows = log_decay.T

    last, crow = last_pieces(doc_lengths, decay_rows, keys, values, members)
    last = swap(last, near)
    side, ccol = side_pieces(doc_lengths, owner_ids, decay_rows, crow, keys, values, members, SIDE, False)
    last, side = lax.optimization_barrier((last, side))
    side = swap(side, near)

    coming = jnp.zeros((hp, 128, 128), BF16)
    for _ in range(quads - 1):
        leaving = leave_quad(doc_lengths, last, coming, rows)
        coming = lax.ppermute(leaving, "seq", onward)
    crow_after, _ = lax.optimization_barrier((crow, leaving))
    local = block_attention(doc_lengths, queries, keys, values, crow_after, ccol)
    over = crowded(doc_lengths, spread, rows, groups)
    device, late = own_final(doc_lengths, owner_ids, rows)
    coming, local, over, device, late = lax.optimization_barrier((coming, local, over, device, late))

    entering = swap(enter_states(doc_lengths, last, coming, rows), near).reshape(heads, 128, 128)
    finals = final_states(doc_lengths, owner_ids, last, side, coming, rows, spread)
    entering, finals = lax.optimization_barrier((entering, finals))
    owned = swap(finals).reshape(quads, heads, 128, 128)
    mixed = mix(doc_lengths, queries, entering, local, gate, gain, ccol)
    owned = lax.dynamic_index_in_dim(owned, device // members, 0, True)

    def send_rest(owned):
        rest, _ = side_pieces(doc_lengths, owner_ids, decay_rows, crow, keys, values, heads, spread, True)
        rest = swap(rest)
        return jnp.where(late, lax.dynamic_index_in_dim(rest, device, 0, True), owned)

    owned = lax.cond(over, send_rest, lambda owned: owned, owned)
    return mixed, owned


def solution(mesh):
    placed = (
        P(("groups", "seq"), "tp"),
        P(("groups", "seq"), "tp"),
        P(("groups", "seq"), "tp"),
        P(("groups", "seq"), "tp"),
        P(("groups", "seq"), "tp"),
        P("tp"),
        P("groups"),
        P("groups"),
    )
    return jax.shard_map(
        functools.partial(on_device, mesh.shape["seq"], mesh.shape["groups"]),
        mesh=mesh,
        in_specs=placed,
        out_specs=(P(("groups", "seq"), "tp"), P(("groups", "seq"), "tp", None, None)),
        check_vma=False,
    )
```

time: 130 us -> 101 us (0.78)
  blocking collectives: 56.9 us -> 0 us
  starting transfers between devices: 9.98 us -> 24.6 us
  between operations: 1.96 us -> 6.88 us
  Pallas kernels: 43.3 us -> 48.1 us
  local copies, waits for them, and re-layouts: 3.01 us -> 7.16 us
  waiting for transfers between devices: 13.6 us -> 10.3 us
  other arithmetic: 0.86 us -> 3.57 us
    all_to_all x1 -> x0, blocking collectives: 56.9 us -> none  [swap(): return lax.all_to_all(x, 'seq', split_axis=0, concat_axis=0, tiled=True)]
    all_to_all x2 -> x4, starting transfers between devices: 7.11 us -> 17.2 us  [swap(): lax.all_to_all(x, 'seq', split_axis=0, concat_axis=0, axis_index_groups=g...]
    pallas_call x4 -> x7, Pallas kernels: 43.3 us -> 48.1 us  [the longest x1 18.5 us: block_attention(): pl.pallas_call(blocks_kernel, grid=(heads // hb,), in_specs=[SMEM, wide,...]
    ppermute x0 -> x1, starting transfers between devices: none -> 4.5 us  [on_device(): coming = lax.ppermute(leaving, 'seq', onward)]
    unnamed x13 -> x18, local copies, waits for them, and re-layouts: 3.01 us -> 7.1 us
    all_to_all x2 -> x4, waiting for transfers between devices: 13.6 us -> 10.3 us  [swap(): lax.all_to_all(x, 'seq', split_axis=0, concat_axis=0, axis_index_groups=g...]
    reduce_sum x0 -> x2, other arithmetic: none -> 2.65 us  [the longest x1 1.9 us: own_final(): ahead = jnp.sum(((source == device) & (index < doc)).astype(jnp.int32))]
  transfers between devices with their start and end apart: 3 -> 6, of which waited for: 1 -> 2; matrix products, arithmetic and copies ran while one was open for 1% -> 4% of each run, Pallas kernels for 23% -> 41%
where the time goes in v2:
time: 101 us
  Pallas kernels  48.1 us (48%)
  starting transfers between devices  24.6 us (24%)
  waiting for transfers between devices  10.3 us (10%)
  local copies, waits for them, and re-layouts  7.16 us (7%)
  between operations  6.88 us (7%)
  other arithmetic  3.57 us (4%)
    pallas_call x1, Pallas kernels, block_attention(): pl.pallas_call(blocks_kernel, grid=(heads // hb,), in_specs=[SMEM, wide,...  18.5 us
    all_to_all x4, starting transfers between devices, swap(): lax.all_to_all(x, 'seq', split_axis=0, concat_axis=0, axis_index_groups=g...  17.2 us
    pallas_call x1, Pallas kernels, mix(): pl.pallas_call(mix_kernel, grid=(heads // hb,), in_specs=[SMEM, wide, pl....  11.7 us
    all_to_all x4, waiting for transfers between devices, swap(): lax.all_to_all(x, 'seq', split_axis=0, concat_axis=0, axis_index_groups=g...  10.3 us
    pallas_call x1, Pallas kernels, side_pieces(): pl.pallas_call(functools.partial(side_kernel, slots, by_owner), grid=(mem...  7.46 us
    unnamed x18, local copies, waits for them, and re-layouts  7.1 us
    pallas_call x1, Pallas kernels, last_pieces(): pl.pallas_call(last_kernel, grid=(members,), in_specs=[SMEM, whole((heads...  6.84 us
    ppermute x1, starting transfers between devices, on_device(): coming = lax.ppermute(leaving, 'seq', onward)  4.5 us
  transfers between devices with their start and end apart: 6, of which 2 were waited for; matrix products, arithmetic and copies ran while one was open for 4% of the time, Pallas kernels for 41%

profile of v2, /device:TPU:0, one launch (start us, length us, event | category | flops | bytes accessed | tf_op | source)
XLA Modules:
  0.0 100.6 jit_solution(9710409934183346491)
XLA Ops:
  0.6 0.0 copy-start.6
  0.6 0.0 copy-start.7
  0.7 0.0 copy-start.8
  0.7 6.8 %last_pieces.1 = (bf16[4,528,128]{2,1,0:T(8,128)(2,1)}, f32[16,1024]{1,0:T(8,128)S(1)}) custom-call(s32[8]{0:T(128)} %len_ref.13, f32[16,1024]{1,0:T(8,128)} %bitcast.7, bf16[1024,2048]{1,0:T(8,128)(2,1)} %k_ref.5, bf16[1024,2048]{1,0:T(8,128)(2,1)} %v_ref.5), custom_call_target="tpu_custom_call" | custom-call | flops 536870912 | bytes 8388608 | tf_op jit(solution)/shard_map/last_pieces/pallas_call | solution.py:121
  7.5 5.2 %all-to-all-start.1 = ((bf16[4,528,128]{2,1,0:T(8,128)(2,1)}), bf16[4,528,128]{2,1,0:T(8,128)(2,1)S(1)}, u32[]{:S(2)}, u32[]{:S(2)}) async-start(bf16[4,528,128]{2,1,0:T(8,128)(2,1)} %get-tuple-element.48), calls=%async_computation.1 | async-start | bytes 1081344 | tf_op jit(solution)/shard_map/all_to_all | solution.py:462
  12.7 0.0 copy-done.6
  12.8 0.0 copy-done.7
  12.8 0.0 copy-done.8
  12.8 7.5 %side_pieces.3 = (bf16[4,1536,128]{2,1,0:T(8,128)(2,1)S(1)}, f32[1024,16]{1,0:T(8,128)S(1)}) custom-call(s32[8]{0:T(128)S(1)} %copy-done.7, s32[8]{0:T(128)S(1)} %copy-done.8, f32[16,1024]{1,0:T(8,128)S(1)} %bitcast.8, f32[16,1024]{1,0:T(8,128)S(1)} %get-tuple-element.52.crow_ref, bf16[1024,2048]{1,0:T(8,128)(2,1)} %k_ref.5, bf16[1024,2048]{1,0:T(8,128)(2,1)} %v_ref.5), custom_call_target="tpu_custom_call" | custom-call | flops 1610612736 | bytes 8388608 | tf_op jit(solution)/shard_map/side_pieces/pallas_call | solution.py:199
  20.2 0.0 copy-start.4
  20.2 1.1 %copy-done.4 = bf16[4,1536,128]{2,1,0:T(8,128)(2,1)} copy-done((bf16[4,1536,128]{2,1,0:T(8,128)(2,1)}, bf16[4,1536,128]{2,1,0:T(8,128)(2,1)S(1)}, u32[]{:S(2)}) %copy-start.4) | copy-done | bytes 1572888
  21.4 0.0 all-to-all-done.1.last_ref
  21.4 4.2 %all-to-all-start.3 = ((bf16[4,1536,128]{2,1,0:T(8,128)(2,1)}), bf16[4,1536,128]{2,1,0:T(8,128)(2,1)S(1)}, u32[]{:S(2)}, u32[]{:S(2)}) async-start(bf16[4,1536,128]{2,1,0:T(8,128)(2,1)} %copy-done.4), calls=%async_computation.3 | async-start | bytes 3145728 | tf_op jit(solution)/shard_map/all_to_all | solution.py:462
  25.6 0.1 select_reduce_fusion
  25.7 0.7 select_reduce_fusion.1
  26.5 0.1 convert_reduce_fusion
  26.6 0.7 reduce_max.9
  27.9 2.9 %collective-permute-start.1 = (f32[1]{0:T(128)}, f32[1]{0:T(128)}, u32[]{:S(2)}, u32[]{:S(2)}) collective-permute-start(f32[1]{0:T(128)} %bitcast.1), channel_id=1, source_target_pairs={{0,16},{16,0},{1,17},{17,1},{2,18},{18,2},{3,19},{19,3},{4,20},{20... | collective-permute-start | bytes 20 | tf_op jit(solution)/shard_map/ppermute | solution.py:473
  31.5 1.9 %fusion.2 = s32[]{:T(128)} fusion(s32[8]{0:T(128)S(1)} %get-tuple-element.65, s32[]{:T(128)} %get-tuple-element.63, s32[]{:T(128)} %get-tuple-element.60), kind=kLoop, calls=%fused_computation.19 | loop fusion | flops 39 | bytes 44 | tf_op jit(solution)/shard_map/reduce_sum | solution.py:484
  34.7 0.0 collective-permute-done.1
  35.3 0.7 leave_quad.1
  36.1 4.5 %collective-permute-start = (bf16[4,128,128]{2,1,0:T(8,128)(2,1)S(1)}, bf16[4,128,128]{2,1,0:T(8,128)(2,1)S(1)}, u32[]{:S(2)}, u32[]{:S(2)}) collective-permute-start(bf16[4,128,128]{2,1,0:T(8,128)(2,1)S(1)} %leave_quad.1), channel_id=1, source_target_pairs={{0,8},{2,10},{4,12},{6,14},{1,9},{3,11},{5,13},{7,15},{16,24},{18,... | collective-permute-start | bytes 393224 | tf_op jit(solution)/shard_map/ppermute | solution.py:507
  40.6 0.0 copy-start
  40.6 2.2 %copy-done = bf16[1024,2048]{1,0:T(8,128)(2,1)S(1)} copy-done((bf16[1024,2048]{1,0:T(8,128)(2,1)S(1)}, bf16[1024,2048]{1,0:T(8,128)(2,1)}, u32[]{:S(2)}) %copy-start) | copy-done | bytes 4194328
  42.8 18.5 %block_attention.1.local_ref = f32[1024,2048]{1,0:T(8,128)} custom-call(s32[8]{0:T(128)S(1)} %copy-done.7, bf16[1024,2048]{1,0:T(8,128)(2,1)S(1)} %copy-done, bf16[1024,2048]{1,0:T(8,128)(2,1)} %k_ref.5, bf16[1024,2048]{1,0:T(8,128)(2,1)} %v_ref.5, f32[16,1024]{1,0:T(8,128)S(1)} %get-tuple-element.52.crow_ref, f32[1024,16]{1,0:T(8,128)S(1)} %get-tuple-element.53.ccol_ref), custom_call_target="tpu_custom_call" | custom-call | flops 4294967296 | bytes 20971520 | tf_op jit(solution)/shard_map/block_attention/pallas_call | solution.py:285
  61.3 0.0 copy-start.9
  61.3 0.0 collective-permute-done.in_ref
  61.3 0.7 enter_states.1
  62.0 0.0 copy-start.3
  62.0 0.8 copy-done.3
  62.8 0.0 all-to-all-done.3.side_ref
  62.8 4.2 %all-to-all-start.2 = ((bf16[4,4,128,128]{3,2,1,0:T(8,128)(2,1)}), bf16[4,4,128,128]{3,2,1,0:T(8,128)(2,1)S(1)}, u32[]{:S(2)}, u32[]{:S(2)}) async-start(bf16[4,4,128,128]{3,2,1,0:T(8,128)(2,1)} %copy-done.3), calls=%async_computation.2 | async-start | bytes 1048576 | tf_op jit(solution)/shard_map/all_to_all | solution.py:462
  67.0 2.2 %final_states.1 = bf16[8,4,128,128]{3,2,1,0:T(8,128)(2,1)} custom-call(s32[8]{0:T(128)S(1)} %copy-done.7, s32[8]{0:T(128)S(1)} %copy-done.8, bf16[4,528,128]{2,1,0:T(8,128)(2,1)S(1)} %all-to-all-done.1.last_ref, bf16[4,1536,128]{2,1,0:T(8,128)(2,1)S(1)} %all-to-all-done.3.side_ref, bf16[4,128,128]{2,1,0:T(8,128)(2,1)S(1)} %collective-permute-done.in_ref), custom_call_target="tpu_custom_call" | custom-call | tf_op jit(solution)/shard_map/final_states/pallas_call | solution.py:406
  69.2 4.4 %all-to-all-done.2 = bf16[4,4,128,128]{3,2,1,0:T(8,128)(2,1)S(1)} async-done(((bf16[4,4,128,128]{3,2,1,0:T(8,128)(2,1)}), bf16[4,4,128,128]{3,2,1,0:T(8,128)(2,1)S(1)}, u32[]{:S(2)}, u32[]{:S(2)}) %all-to-all-start.2) | async-done | bytes 524320 | tf_op jit(solution)/shard_map/all_to_all | solution.py:462
  73.6 3.6 %all-to-all-start.4 = ((bf16[8,4,128,128]{3,2,1,0:T(8,128)(2,1)}), bf16[8,4,128,128]{3,2,1,0:T(8,128)(2,1)S(1)}, u32[]{:S(2)}, u32[]{:S(2)}) async-start(bf16[8,4,128,128]{3,2,1,0:T(8,128)(2,1)} %final_states.1), calls=%async_computation.4 | async-start | bytes 2097152 | tf_op jit(solution)/shard_map/all_to_all | solution.py:462
  77.2 0.0 copy-done.9
  80.0 0.0 copy-start.1
  80.0 2.2 %copy-done.1 = bf16[1024,2048]{1,0:T(8,128)(2,1)S(1)} copy-done((bf16[1024,2048]{1,0:T(8,128)(2,1)S(1)}, bf16[1024,2048]{1,0:T(8,128)(2,1)}, u32[]{:S(2)}) %copy-start.1) | copy-done | bytes 4194328
  82.2 11.7 %mix.1 = bf16[1024,2048]{1,0:T(8,128)(2,1)} custom-call(s32[8]{0:T(128)S(1)} %copy-done.7, bf16[1024,2048]{1,0:T(8,128)(2,1)S(1)} %copy-done.1, bf16[16,128,128]{2,1,0:T(8,128)(2,1)S(1)} %bitcast.5, f32[1024,2048]{1,0:T(8,128)} %block_attention.1.local_ref, bf16[1024,2048]{1,0:T(8,128)(2,1)} %gate_ref.1, bf16[1,2048]{1,0:T(2,128)(2,1)S(1)} %reshape.74.gain_ref, ...), custom_call_target="tpu_custom_call" | custom-call | flops 536870912 | bytes 20971520 | tf_op jit(solution)/shard_map/mix/pallas_call | solution.py:439
  93.8 5.9 %all-to-all-done.4 = bf16[8,4,128,128]{3,2,1,0:T(8,128)(2,1)S(1)} async-done(((bf16[8,4,128,128]{3,2,1,0:T(8,128)(2,1)}), bf16[8,4,128,128]{3,2,1,0:T(8,128)(2,1)S(1)}, u32[]{:S(2)}, u32[]{:S(2)}) %all-to-all-start.4) | async-done | bytes 1048608 | tf_op jit(solution)/shard_map/all_to_all | solution.py:462
  99.8 0.0 copy-start.5
  99.8 0.8 copy-done.5
  (5 shorter events, 0.1 us)
Async XLA Ops:
  0.6 12.1 %copy-start.6 = (f32[1024,16]{0,1:T(8,128)S(1)}, f32[1024,16]{0,1:T(8,128)}, u32[]{:S(2)}) copy-start(f32[1024,16]{0,1:T(8,128)} %param.13) | copy-start | bytes 196612
  0.6 12.1 %copy-start.7 = (s32[8]{0:T(128)S(1)}, s32[8]{0:T(128)}, u32[]{:S(2)}) copy-start(s32[8]{0:T(128)} %len_ref.13) | copy-start | bytes 100
  0.7 12.1 %copy-start.8 = (s32[8]{0:T(128)S(1)}, s32[8]{0:T(128)}, u32[]{:S(2)}) copy-start(s32[8]{0:T(128)} %own_ref.3) | copy-start | bytes 100
  7.5 13.9 %all-to-all-start.1 = ((bf16[4,528,128]{2,1,0:T(8,128)(2,1)}), bf16[4,528,128]{2,1,0:T(8,128)(2,1)S(1)}, u32[]{:S(2)}, u32[]{:S(2)}) async-start(bf16[4,528,128]{2,1,0:T(8,128)(2,1)} %get-tuple-element.48), calls=%async_computation.1 | async-start | bytes 1081344 | tf_op jit(solution)/shard_map/all_to_all | solution.py:462
  20.2 1.1 %copy-start.4 = (bf16[4,1536,128]{2,1,0:T(8,128)(2,1)}, bf16[4,1536,128]{2,1,0:T(8,128)(2,1)S(1)}, u32[]{:S(2)}) copy-start(bf16[4,1536,128]{2,1,0:T(8,128)(2,1)S(1)} %get-tuple-element.55) | copy-start | bytes 4718596
  21.4 41.4 %all-to-all-start.3 = ((bf16[4,1536,128]{2,1,0:T(8,128)(2,1)}), bf16[4,1536,128]{2,1,0:T(8,128)(2,1)S(1)}, u32[]{:S(2)}, u32[]{:S(2)}) async-start(bf16[4,1536,128]{2,1,0:T(8,128)(2,1)} %copy-done.4), calls=%async_computation.3 | async-start | bytes 3145728 | tf_op jit(solution)/shard_map/all_to_all | solution.py:462
  27.9 6.7 %collective-permute-start.1 = (f32[1]{0:T(128)}, f32[1]{0:T(128)}, u32[]{:S(2)}, u32[]{:S(2)}) collective-permute-start(f32[1]{0:T(128)} %bitcast.1), channel_id=1, source_target_pairs={{0,16},{16,0},{1,17},{17,1},{2,18},{18,2},{3,19},{19,3},{4,20},{20... | collective-permute-start | bytes 20 | tf_op jit(solution)/shard_map/ppermute | solution.py:473
  36.1 25.2 %collective-permute-start = (bf16[4,128,128]{2,1,0:T(8,128)(2,1)S(1)}, bf16[4,128,128]{2,1,0:T(8,128)(2,1)S(1)}, u32[]{:S(2)}, u32[]{:S(2)}) collective-permute-start(bf16[4,128,128]{2,1,0:T(8,128)(2,1)S(1)} %leave_quad.1), channel_id=1, source_target_pairs={{0,8},{2,10},{4,12},{6,14},{1,9},{3,11},{5,13},{7,15},{16,24},{18,... | collective-permute-start | bytes 393224 | tf_op jit(solution)/shard_map/ppermute | solution.py:507
  40.6 2.2 %copy-start = (bf16[1024,2048]{1,0:T(8,128)(2,1)S(1)}, bf16[1024,2048]{1,0:T(8,128)(2,1)}, u32[]{:S(2)}) copy-start(bf16[1024,2048]{1,0:T(8,128)(2,1)} %q_ref.3) | copy-start | bytes 12582916
  61.3 15.9 %copy-start.9 = (bf16[2048]{0:T(1024)(128)(2,1)S(1)}, bf16[2048]{0:T(1024)(128)(2,1)}, u32[]{:S(2)}) copy-start(bf16[2048]{0:T(1024)(128)(2,1)} %param.15) | copy-start | bytes 12292
  62.0 0.8 copy-start.3
  62.8 10.8 %all-to-all-start.2 = ((bf16[4,4,128,128]{3,2,1,0:T(8,128)(2,1)}), bf16[4,4,128,128]{3,2,1,0:T(8,128)(2,1)S(1)}, u32[]{:S(2)}, u32[]{:S(2)}) async-start(bf16[4,4,128,128]{3,2,1,0:T(8,128)(2,1)} %copy-done.3), calls=%async_computation.2 | async-start | bytes 1048576 | tf_op jit(solution)/shard_map/all_to_all | solution.py:462
  73.6 26.1 %all-to-all-start.4 = ((bf16[8,4,128,128]{3,2,1,0:T(8,128)(2,1)}), bf16[8,4,128,128]{3,2,1,0:T(8,128)(2,1)S(1)}, u32[]{:S(2)}, u32[]{:S(2)}) async-start(bf16[8,4,128,128]{3,2,1,0:T(8,128)(2,1)} %final_states.1), calls=%async_computation.4 | async-start | bytes 2097152 | tf_op jit(solution)/shard_map/all_to_all | solution.py:462
  80.0 2.2 %copy-start.1 = (bf16[1024,2048]{1,0:T(8,128)(2,1)S(1)}, bf16[1024,2048]{1,0:T(8,128)(2,1)}, u32[]{:S(2)}) copy-start(bf16[1024,2048]{1,0:T(8,128)(2,1)} %q_ref.3) | copy-start | bytes 12582916
  99.8 0.8 copy-start.5

commit v3 on v2

v3 whole, which is shorter than its diff:
```python
import functools
import math

import jax
import jax.numpy as jnp
from jax import lax
from jax.experimental import pallas as pl
from jax.experimental.pallas import tpu as pltpu
from jax.sharding import PartitionSpec as P

BLK = 512
SIDE = 3
EXTRA = 16
CHUNK = 256
EARLY = 6
NEG = -1e30
LOG2E = math.log2(math.e)
SCALE = 128**-0.5
F32, BF16 = jnp.float32, jnp.bfloat16
SMEM = pl.BlockSpec(memory_space=pltpu.SMEM)
VMEM = pl.BlockSpec(memory_space=pltpu.VMEM)
LIMIT = pltpu.CompilerParams(vmem_limit_bytes=60 * 2**20)


def dot(a, b, contract=((1,), (0,))):
    return lax.dot_general(a, b, (contract, ((), ())), preferred_element_type=F32)


def iota(shape, dim):
    return lax.broadcasted_iota(jnp.int32, shape, dim)


def read_ends(len_ref, count):
    ends, total = [], jnp.int32(0)
    for d in range(count):
        total = total + len_ref[d]
        ends.append(total)
    return ends


def run_end(ends, pos):
    best = ends[-1]
    for e in reversed(ends[:-1]):
        best = jnp.where(e > pos, e, best)
    return best


def run_start(ends, pos):
    best = jnp.zeros_like(pos)
    for e in ends[:-1]:
        best = jnp.where(e <= pos, e, best)
    return best


def split3(x):
    hi = x.astype(BF16)
    rest = x - hi.astype(F32)
    mid = rest.astype(BF16)
    return hi, mid, (rest - mid.astype(F32)).astype(BF16)


def cum_rows(ld_ref, crow_ref):
    heads, rows = ld_ref.shape
    upper = (iota((BLK, BLK), 0) <= iota((BLK, BLK), 1)).astype(F32).astype(BF16)
    base = jnp.zeros((heads, 1), F32)
    for b in range(rows // BLK):
        part = ld_ref[:, b * BLK : (b + 1) * BLK] * LOG2E
        sums = dot(jnp.concatenate(split3(part), axis=0), upper)
        row = sums[2 * heads :] + sums[heads : 2 * heads] + sums[:heads] + base
        crow_ref[:, b * BLK : (b + 1) * BLK] = row
        base = row[:, BLK - 1 :]


def value_at(cum, at, index):
    return jnp.sum(jnp.where(at == index, cum, 0.0), axis=1, keepdims=True)


def span_weights(cum, at, low, high):
    inside = (at >= low) & (at <= high)
    return jnp.exp2(jnp.where(inside, value_at(cum, at, high) - cum, NEG) + math.log2(SCALE))


def weigh(keys, w_ref, h):
    flipped = keys.T.astype(F32)
    weights = [jnp.broadcast_to(w_ref[pl.ds(h + j, 1), :], (128, keys.shape[0])) for j in range(2)]
    return (flipped * jnp.concatenate(weights, axis=0)).astype(BF16)


def last_kernel(len_ref, ld_ref, k_ref, v_ref, out_ref, crow_ref, w_ref, first_ref):
    heads, rows = ld_ref.shape
    step = pl.program_id(0)
    hp = k_ref.shape[1] // 128

    @pl.when(step == 0)
    def _():
        cum_rows(ld_ref, crow_ref)
        first = lax.axis_index("seq") * rows
        ends = read_ends(len_ref, len_ref.shape[0])
        at = iota((heads, rows), 1)
        cum = crow_ref[...]
        low = jnp.maximum(run_start(ends, first + rows - 1) - first, 0)
        w_ref[...] = span_weights(cum, at, low, rows - 1)
        stop = jnp.minimum(run_end(ends, first) - 1 - first, rows - 1)
        goes_on = (run_start(ends, first) < first).astype(F32)
        first_ref[...] = jnp.broadcast_to(jnp.exp2(value_at(cum, at, stop)) * goes_on, (heads, 128))

    for i in range(0, hp, 2):
        lanes = slice(i * 128, (i + 2) * 128)
        states = dot(weigh(k_ref[:, lanes], w_ref, step * hp + i), v_ref[:, lanes])
        out_ref[0, i * 128 : (i + 1) * 128, :] = states[:128, :128].astype(BF16)
        out_ref[0, (i + 1) * 128 : (i + 2) * 128, :] = states[128:, 128:].astype(BF16)
    rate = first_ref[pl.ds(step * hp, hp), :]
    high = rate.astype(BF16).astype(F32)
    pad = jnp.zeros((EXTRA - 2 * hp, 128), F32)
    out_ref[0, hp * 128 :, :] = jnp.concatenate([high, rate - high, pad], axis=0).astype(BF16)


def whole(shape):
    return pl.BlockSpec(shape, lambda j: (0,) * len(shape))


def last_pieces(doc_lengths, decay_rows, keys, values, members):
    heads, rows = decay_rows.shape
    hp = heads // members
    wide = pl.BlockSpec((rows, hp * 128), lambda j: (0, j))
    size = hp * 128 + EXTRA
    return pl.pallas_call(
        last_kernel,
        grid=(members,),
        in_specs=[SMEM, whole((heads, rows)), wide, wide],
        out_specs=[pl.BlockSpec((1, size, 128), lambda j: (j, 0, 0)), whole((heads, rows))],
        out_shape=[
            jax.ShapeDtypeStruct((members, size, 128), BF16),
            jax.ShapeDtypeStruct((heads, rows), F32),
        ],
        scratch_shapes=[pltpu.VMEM((heads, rows), F32), pltpu.VMEM((heads, 128), F32)],
        compiler_params=LIMIT,
        cost_estimate=pl.CostEstimate(
            flops=heads * rows * 128 * 256, bytes_accessed=rows * heads * 128 * 4, transcendentals=heads * rows
        ),
        name="last_pieces",
    )(doc_lengths, decay_rows, keys, values)


def side_kernel(slots, by_owner, len_ref, own_ref, ld_ref, crow_ref, k_ref, v_ref, out_ref, ccol_ref, flag_ref, w_ref, keep_ref):
    heads, rows = crow_ref.shape
    step = pl.program_id(0)
    hp = k_ref.shape[1] // 128

    @pl.when(step == 0)
    def _():
        lower = (iota((BLK, BLK), 0) >= iota((BLK, BLK), 1)).astype(F32).astype(BF16)
        base = jnp.zeros((1, heads), F32)
        for b in range(rows // BLK):
            part = ld_ref[:, b * BLK : (b + 1) * BLK] * LOG2E
            col = jnp.zeros((BLK, heads), F32)
            for piece in reversed(split3(part)):
                col = col + dot(lower, piece, ((1,), (1,)))
            col = col + base
            ccol_ref[b * BLK : (b + 1) * BLK, :] = col
            base = col[BLK - 1 :, :]
        me = lax.axis_index("seq")
        first = me * rows
        last = first + rows - 1
        ends = read_ends(len_ref, len_ref.shape[0])
        starts = [jnp.int32(0)] + ends[:-1]
        lows = [jnp.int32(0)] * slots
        highs = [jnp.int32(-1)] * slots
        place, rank, previous = jnp.int32(0), jnp.int32(0), jnp.int32(-1)
        crowded, owned_in, owned_late = jnp.int32(0), jnp.int32(0), jnp.int32(0)
        for d in range(len(ends)):
            here = (ends[d] > first) & (ends[d] <= last)
            low = jnp.maximum(starts[d] - first, 0)
            for s in range(slots):
                mine = here & ((place >= SIDE) & (own_ref[d] == s) if by_owner else (place == s))
                lows[s] = jnp.where(mine, low, lows[s])
                highs[s] = jnp.where(mine, ends[d] - 1 - first, highs[s])
            place = place + here.astype(jnp.int32)
            device = (ends[d] - 1) // rows
            rank = jnp.where(device == previous, rank + 1, 0)
            previous = device
            late = ((rank >= SIDE) & (ends[d] != (device + 1) * rows)).astype(jnp.int32)
            crowded = jnp.maximum(crowded, late)
            owned_in = jnp.where(own_ref[d] == me, device, owned_in)
            owned_late = jnp.where(own_ref[d] == me, late, owned_late)
        flag_ref[0] = owned_in
        flag_ref[1] = owned_late
        flag_ref[2] = crowded
        at = iota((heads, rows), 1)
        cum = crow_ref[...]
        row_at = iota((16, rows), 1)
        total = jnp.zeros((heads, rows), F32)
        for s in range(slots):
            total = total + span_weights(cum, at, lows[s], highs[s])
            inside = (row_at >= lows[s]) & (row_at <= highs[s])
            keep_ref[s] = jnp.where(inside, 1.0, 0.0).astype(BF16)
        w_ref[...] = total

    for i in range(0, hp, 2):
        lanes = slice(i * 128, (i + 2) * 128)
        weighted = weigh(k_ref[:, lanes], w_ref, step * hp + i).reshape(16, 16, rows)
        for s in range(slots):
            kept = (weighted * keep_ref[s][None]).reshape(256, rows)
            states = dot(kept, v_ref[:, lanes])
            for j in range(2):
                state = states[j * 128 : (j + 1) * 128, j * 128 : (j + 1) * 128].astype(BF16)
                if by_owner:
                    out_ref[s, i + j] = state
                else:
                    at = (s * hp + i + j) * 128
                    out_ref[0, at : at + 128, :] = state


def side_pieces(doc_lengths, owner_ids, decay_rows, crow, keys, values, members, slots, by_owner):
    heads, rows = crow.shape
    hp = heads // members
    wide = pl.BlockSpec((rows, hp * 128), lambda j: (0, j))
    if by_owner:
        out = jax.ShapeDtypeStruct((slots, heads, 128, 128), BF16)
        out_spec = pl.BlockSpec((slots, hp, 128, 128), lambda j: (0, j, 0, 0))
    else:
        out = jax.ShapeDtypeStruct((members, slots * hp * 128, 128), BF16)
        out_spec = pl.BlockSpec((1, slots * hp * 128, 128), lambda j: (j, 0, 0))
    return pl.pallas_call(
        functools.partial(side_kernel, slots, by_owner),
        grid=(members,),
        in_specs=[SMEM, SMEM, whole((heads, rows)), whole((heads, rows)), wide, wide],
        out_specs=[out_spec, whole((rows, heads)), SMEM],
        out_shape=[out, jax.ShapeDtypeStruct((rows, heads), F32), jax.ShapeDtypeStruct((4,), jnp.int32)],
        scratch_shapes=[pltpu.VMEM((heads, rows), F32), pltpu.VMEM((slots, 16, rows), BF16)],
        compiler_params=LIMIT,
        cost_estimate=pl.CostEstimate(
            flops=slots * heads * rows * 128 * 256, bytes_accessed=rows * heads * 128 * 4, transcendentals=heads * rows
        ),
        name="side_pieces",
    )(doc_lengths, owner_ids, decay_rows, crow, keys, values)


def head_column(ccol_ref, h):
    cols = ccol_ref[...]
    return jnp.sum(jnp.where(iota(cols.shape, 1) == h, cols, 0.0), axis=1, keepdims=True)


def fill_bias(first, ends, bias_ref):
    for c in range(bias_ref.shape[0] // CHUNK):
        base = first + c * CHUNK
        t_pos = base + iota((CHUNK, 1), 0)
        start = run_start(ends, t_pos)
        s_pos = base + iota((CHUNK, CHUNK), 1)
        keep = (s_pos <= t_pos) & (s_pos >= start)
        bias_ref[c * CHUNK : (c + 1) * CHUNK, :] = jnp.where(keep, math.log2(SCALE), NEG)


def attend(first, ends, q_ref, k_ref, v_ref, lanes, row_all, col_all, bias_ref, state, emit):
    rows = q_ref.shape[0]
    half = CHUNK // 2
    for c in range(rows // CHUNK):
        r0 = c * CHUNK
        key = k_ref[r0 : r0 + CHUNK, lanes]
        value = v_ref[r0 : r0 + CHUNK, lanes]
        row = row_all[:, r0 : r0 + CHUNK]
        base = row_all[:, r0 - 1 : r0] if c else jnp.zeros((1, 1), F32)
        reach = run_end(ends, first + r0 - 1) - (first + r0)
        state_bf = None if state is None else state.astype(BF16)
        for part in range(2):
            t0 = r0 + part * half
            width = (part + 1) * half
            query = q_ref[t0 : t0 + half, lanes]
            col = col_all[t0 : t0 + half]
            scores = dot(query, key[:width], ((1,), (1,)))
            decay = jnp.exp2((col - row[:, :width]) + bias_ref[t0 : t0 + half, :width])
            att = dot((scores * decay).astype(BF16), value[:width])
            if state is not None:
                at = part * half + iota((half, 1), 0)
                lead = jnp.exp2(jnp.where(at < reach, col - base, NEG))
                att = att + lead * dot(query, state_bf)
            emit(t0, half, att)
        if r0 + CHUNK < rows:
            since = run_start(ends, first + r0 + CHUNK - 1) - (first + r0)
            total = row[:, CHUNK - 1 :]
            inside = iota((1, CHUNK), 1) >= since
            weight = jnp.exp2(jnp.where(inside, total - row, NEG) + math.log2(SCALE))
            fresh = dot((key.T.astype(F32) * weight).astype(BF16), value)
            if state is not None:
                fresh = fresh + state * jnp.exp2(jnp.where(CHUNK <= reach, total - base, NEG))
            state = fresh


def early_kernel(len_ref, q_ref, k_ref, v_ref, crow_ref, ccol_ref, out_ref, bias_ref):
    rows = q_ref.shape[0]
    step = pl.program_id(0)
    first = lax.axis_index("seq") * rows
    ends = read_ends(len_ref, len_ref.shape[0])

    @pl.when(step == 0)
    def _():
        fill_bias(first, ends, bias_ref)

    for i in range(2):
        h = step * 2 + i
        lanes = slice(i * 128, (i + 1) * 128)

        def emit(t0, size, att):
            out_ref[t0 : t0 + size, lanes] = att

        attend(
            first, ends, q_ref, k_ref, v_ref, lanes, crow_ref[pl.ds(h, 1), :], head_column(ccol_ref, h), bias_ref, None, emit
        )


def early_attention(doc_lengths, queries, keys, values, crow, ccol):
    heads, rows = crow.shape
    wide = pl.BlockSpec((rows, 256), lambda j: (0, j))
    return pl.pallas_call(
        early_kernel,
        grid=(EARLY // 2,),
        in_specs=[SMEM, wide, wide, wide, whole((heads, rows)), whole((rows, heads))],
        out_specs=wide,
        out_shape=jax.ShapeDtypeStruct((rows, EARLY * 128), F32),
        scratch_shapes=[pltpu.VMEM((rows, CHUNK), F32)],
        compiler_params=LIMIT,
        cost_estimate=pl.CostEstimate(
            flops=EARLY * rows * CHUNK * 128 * 8, bytes_accessed=rows * EARLY * 128 * 10, transcendentals=EARLY * rows * CHUNK
        ),
        name="early_attention",
    )(doc_lengths, queries, keys, values, crow, ccol)


def decay_of(last_ref, e, i, hp):
    extra = last_ref[e, hp * 128 :, :].astype(F32)
    return extra[i : i + 1, :] + extra[hp + i : hp + i + 1, :]


def scan_quad(rows, len_ref, last_ref, state, i, hp, note):
    members = last_ref.shape[0]
    ends = read_ends(len_ref, len_ref.shape[0])
    base = lax.axis_index("seq") // members * members
    for e in range(members):
        note(e, state)
        low = (base + e) * rows
        inner = jnp.int32(0)
        for end in ends:
            inner = inner + ((end > low) & (end < low + rows)).astype(jnp.int32)
        passes = (inner == 0).astype(F32)
        piece = last_ref[e, i * 128 : (i + 1) * 128, :].astype(F32)
        state = state * (decay_of(last_ref, e, i, hp) * passes) + piece
    return state


def leave_kernel(rows, len_ref, last_ref, in_ref, out_ref):
    hp = in_ref.shape[0]
    for i in range(hp):
        state = scan_quad(rows, len_ref, last_ref, in_ref[i].astype(F32), i, hp, lambda e, x: None)
        out_ref[i] = state.astype(BF16)


def leave_quad(doc_lengths, last, coming, rows):
    return pl.pallas_call(
        functools.partial(leave_kernel, rows),
        in_specs=[SMEM, VMEM, VMEM],
        out_specs=VMEM,
        out_shape=jax.ShapeDtypeStruct(coming.shape, BF16),
        compiler_params=LIMIT,
        name="leave_quad",
    )(doc_lengths, last, coming)


def enter_kernel(rows, len_ref, last_ref, in_ref, out_ref):
    hp = in_ref.shape[0]

    def note(i, e, state):
        out_ref[e, i] = state.astype(BF16)

    for i in range(hp):
        scan_quad(rows, len_ref, last_ref, in_ref[i].astype(F32), i, hp, functools.partial(note, i))


def enter_states(doc_lengths, last, coming, rows):
    return pl.pallas_call(
        functools.partial(enter_kernel, rows),
        in_specs=[SMEM, VMEM, VMEM],
        out_specs=VMEM,
        out_shape=jax.ShapeDtypeStruct((last.shape[0],) + coming.shape, BF16),
        compiler_params=LIMIT,
        name="enter_states",
    )(doc_lengths, last, coming)


def final_kernel(rows, len_ref, own_ref, last_ref, side_ref, in_ref, out_ref, state_ref):
    hp = in_ref.shape[0]
    members = last_ref.shape[0]
    ends = read_ends(len_ref, len_ref.shape[0])
    base = lax.axis_index("seq") // members * members

    def note(i, e, state):
        state_ref[e, i] = state

    for i in range(hp):
        scan_quad(rows, len_ref, last_ref, in_ref[i].astype(F32), i, hp, functools.partial(note, i))
    out_ref[...] = jnp.zeros_like(out_ref)
    place, previous = jnp.int32(0), jnp.int32(-1)
    for d in range(len(ends)):
        device = (ends[d] - 1) // rows
        place = jnp.where(device == previous, place + 1, 0)
        previous = device
        at_end = ends[d] == (device + 1) * rows
        enters = (place == 0).astype(F32)
        mine = device // members * members == base
        e = device - base

        def put(i, local):
            state = local.astype(F32) + state_ref[e, i] * (decay_of(last_ref, e, i, hp) * enters)
            out_ref[own_ref[d], i] = state.astype(BF16)

        @pl.when(mine & at_end)
        def _():
            for i in range(hp):
                put(i, last_ref[e, i * 128 : (i + 1) * 128, :])

        @pl.when(mine & jnp.logical_not(at_end))
        def _():
            for i in range(hp):
                row = pl.multiple_of((jnp.minimum(place, SIDE - 1) * hp + i) * 128, 128)
                put(i, side_ref[e, pl.ds(row, 128), :])


def final_states(doc_lengths, owner_ids, last, side, coming, rows, spread):
    return pl.pallas_call(
        functools.partial(final_kernel, rows),
        in_specs=[SMEM, SMEM, VMEM, VMEM, VMEM],
        out_specs=VMEM,
        out_shape=jax.ShapeDtypeStruct((spread,) + coming.shape, BF16),
        scratch_shapes=[pltpu.VMEM((last.shape[0],) + coming.shape, F32)],
        compiler_params=LIMIT,
        name="final_states",
    )(doc_lengths, owner_ids, last, side, coming)


def finish_kernel(
    len_ref, q_ref, k_ref, v_ref, enter_ref, local_ref, gate_ref, gain_ref, crow_ref, ccol_ref, out_ref, bias_ref
):
    rows = q_ref.shape[0]
    step = pl.program_id(0)
    first = lax.axis_index("seq") * rows
    ends = read_ends(len_ref, len_ref.shape[0])

    def emit(lanes, t0, size, att):
        mean = jnp.mean(att * att, axis=1, keepdims=True)
        gate = 1.0 / (1.0 + jnp.exp(-gate_ref[t0 : t0 + size, lanes].astype(F32)))
        gain = gain_ref[:, lanes].astype(F32)
        out_ref[t0 : t0 + size, lanes] = (att * lax.rsqrt(mean + 1e-06) * gain * gate).astype(BF16)

    @pl.when(step == 0)
    def _():
        fill_bias(first, ends, bias_ref)

    @pl.when(step < EARLY // 2)
    def _():
        reach = run_end(ends, first - 1) - first
        for i in range(2):
            lanes = slice(i * 128, (i + 1) * 128)
            col_all = head_column(ccol_ref, step * 2 + i)
            for t0 in range(0, rows, CHUNK):
                at = t0 + iota((CHUNK, 1), 0)
                lead = jnp.exp2(jnp.where(at < reach, col_all[t0 : t0 + CHUNK], NEG))
                carry = dot(q_ref[t0 : t0 + CHUNK, lanes], enter_ref[i])
                emit(lanes, t0, CHUNK, local_ref[t0 : t0 + CHUNK, lanes] + lead * carry)

    @pl.when(step >= EARLY // 2)
    def _():
        for i in range(2):
            h = step * 2 + i
            lanes = slice(i * 128, (i + 1) * 128)
            row_all, col_all = crow_ref[pl.ds(h, 1), :], head_column(ccol_ref, h)
            state = enter_ref[i].astype(F32)
            attend(
                first, ends, q_ref, k_ref, v_ref, lanes, row_all, col_all, bias_ref, state, functools.partial(emit, lanes)
            )


def finish(doc_lengths, queries, keys, values, entering, local, gate, gain, crow, ccol):
    heads, rows = crow.shape
    pairs = EARLY // 2
    wide = pl.BlockSpec((rows, 256), lambda j: (0, j))
    late = pl.BlockSpec((rows, 256), lambda j: (0, jnp.maximum(j, pairs)))
    return pl.pallas_call(
        finish_kernel,
        grid=(heads // 2,),
        in_specs=[
            SMEM,
            wide,
            late,
            late,
            pl.BlockSpec((2, 128, 128), lambda j: (j, 0, 0)),
            pl.BlockSpec((rows, 256), lambda j: (0, jnp.minimum(j, pairs - 1))),
            wide,
            pl.BlockSpec((1, 256), lambda j: (0, j)),
            whole((heads, rows)),
            whole((rows, heads)),
        ],
        out_specs=wide,
        out_shape=jax.ShapeDtypeStruct((rows, heads * 128), BF16),
        scratch_shapes=[pltpu.VMEM((rows, CHUNK), F32)],
        compiler_params=LIMIT,
        cost_estimate=pl.CostEstimate(
            flops=heads * rows * CHUNK * 128 * 8, bytes_accessed=rows * heads * 128 * 10, transcendentals=heads * rows * CHUNK
        ),
        name="finish",
    )(doc_lengths, queries, keys, values, entering, local, gate, gain.reshape(1, -1), crow, ccol)


def pick_kernel(quad_ref, late_ref, in_ref, rest_ref, out_ref):
    out_ref[...] = in_ref[...]

    @pl.when(late_ref[0] > 0)
    def _():
        out_ref[...] = rest_ref[...]


def pick_owned(quad, late, arrived, rest):
    shape = rest.shape
    block = lambda index: pl.BlockSpec(shape, index)
    return pl.pallas_call(
        pick_kernel,
        grid_spec=pltpu.PrefetchScalarGridSpec(
            num_scalar_prefetch=2,
            grid=(1,),
            in_specs=[block(lambda j, quad, late: (quad[0], 0, 0, 0)), block(lambda j, quad, late: (0, 0, 0, 0))],
            out_specs=block(lambda j, quad, late: (0, 0, 0, 0)),
        ),
        out_shape=jax.ShapeDtypeStruct(shape, BF16),
        compiler_params=LIMIT,
        name="pick_owned",
    )(quad, late, arrived, rest)


def swap(x, groups=None):
    return lax.all_to_all(x, "seq", split_axis=0, concat_axis=0, axis_index_groups=groups, tiled=True)


def on_device(spread, queries, keys, values, log_decay, gate, gain, doc_lengths, owner_ids):
    rows, heads = log_decay.shape
    members = 4
    quads = spread // members
    hp = heads // members
    near = [[q * members + m for m in range(members)] for q in range(quads)]
    onward = [(s, s + members) for s in range(spread - members)]
    decay_rows = log_decay.T

    last, crow = last_pieces(doc_lengths, decay_rows, keys, values, members)
    last = swap(last, near)
    side, ccol, flags = side_pieces(doc_lengths, owner_ids, decay_rows, crow, keys, values, members, SIDE, False)
    last, side = lax.optimization_barrier((last, side))
    side = swap(side, near)

    coming = jnp.zeros((hp, 128, 128), BF16)
    for _ in range(quads - 1):
        leaving = leave_quad(doc_lengths, last, coming, rows)
        coming = lax.ppermute(leaving, "seq", onward)
    crow_after, _ = lax.optimization_barrier((crow, leaving))
    local = early_attention(doc_lengths, queries, keys, values, crow_after, ccol)

    def send_rest():
        rest, _, _ = side_pieces(
            doc_lengths, owner_ids, decay_rows, crow_after, keys, values, heads // 2, spread, True
        )
        return lax.dynamic_index_in_dim(swap(rest), flags[0], 0, True)

    rest = lax.cond(flags[2] > 0, send_rest, lambda: jnp.zeros((1, heads, 128, 128), BF16))
    coming, local, rest = lax.optimization_barrier((coming, local, rest))

    entering = swap(enter_states(doc_lengths, last, coming, rows), near).reshape(heads, 128, 128)
    finals = final_states(doc_lengths, owner_ids, last, side, coming, rows, spread)
    arrived = swap(finals).reshape(quads, heads, 128, 128)
    entering, _ = lax.optimization_barrier((entering, finals))
    mixed = finish(doc_lengths, queries, keys, values, entering, local, gate, gain, crow, ccol)
    owned = pick_owned((flags[0] // members).reshape(1), flags[1].reshape(1), arrived, rest)
    return mixed, owned


def solution(mesh):
    placed = (
        P(("groups", "seq"), "tp"),
        P(("groups", "seq"), "tp"),
        P(("groups", "seq"), "tp"),
        P(("groups", "seq"), "tp"),
        P(("groups", "seq"), "tp"),
        P("tp"),
        P("groups"),
        P("groups"),
    )
    return jax.shard_map(
        functools.partial(on_device, mesh.shape["seq"]),
        mesh=mesh,
        in_specs=placed,
        out_specs=(P(("groups", "seq"), "tp"), P(("groups", "seq"), "tp", None, None)),
        check_vma=False,
    )
```

time: 101 us -> 94.5 us (0.936)
  Pallas kernels: 48.1 us -> 52.6 us
  other arithmetic: 3.57 us -> 0 us
  local copies, waits for them, and re-layouts: 7.16 us -> 3.92 us
  between operations: 6.88 us -> 3.93 us
  starting transfers between devices: 24.6 us -> 22.7 us
    unnamed x18 -> x20, local copies, waits for them, and re-layouts: 7.1 us -> 1.84 us
    ppermute x1, waiting for transfers between devices: 0.01 us -> 4.75 us  [on_device(): coming = lax.ppermute(leaving, 'seq', onward)]
    all_to_all x4, waiting for transfers between devices: 10.3 us -> 5.85 us  [swap(): lax.all_to_all(x, 'seq', split_axis=0, concat_axis=0, axis_index_groups=g...]
    reduce_sum x4 -> x0, other arithmetic: 2.88 us -> none  [the longest x1 1.9 us: own_final(): ahead = jnp.sum(((source == device) & (index < doc)).astype(jnp.int32))]
    ppermute x1 -> x0, starting transfers between devices: 2.85 us -> none  [crowded(): lax.ppermute(over, 'groups', [(g, (g + shift) % groups) for g in range(gr...]
    pallas_call x1, Pallas kernels: 0.69 us -> 2.02 us  [enter_states(): pl.pallas_call(functools.partial(enter_kernel, rows), in_specs=[SMEM, VME...]
    pallas_call x1, Pallas kernels: 0.74 us -> 1.93 us  [leave_quad(): pl.pallas_call(functools.partial(leave_kernel, rows), in_specs=[SMEM, VME...]
    all_to_all x4, starting transfers between devices: 17.2 us -> 18.3 us  [swap(): lax.all_to_all(x, 'seq', split_axis=0, concat_axis=0, axis_index_groups=g...]
  transfers between devices with their start and end apart: 6 -> 5, of which waited for: 2 -> 3; matrix products, arithmetic and copies ran while one was open for 4% -> 1% of each run, Pallas kernels for 41% -> 44%
where the time goes in v3:
time: 94.5 us; the launch traced here: 93.8 us
  Pallas kernels  52.6 us (56%)
  starting transfers between devices  22.7 us (24%)
  waiting for transfers between devices  10.6 us (11%)
  between operations  3.93 us (4%)
  local copies, waits for them, and re-layouts  3.92 us (4%)
    all_to_all x4, starting transfers between devices, swap(): lax.all_to_all(x, 'seq', split_axis=0, concat_axis=0, axis_index_groups=g...  18.3 us
    pallas_call x1, Pallas kernels, finish(): pl.pallas_call(finish_kernel, grid=(heads // 2,), in_specs=[SMEM, wide, l...  18 us
    pallas_call x1, Pallas kernels, early_attention(): pl.pallas_call(early_kernel, grid=(EARLY // 2,), in_specs=[SMEM, wide, wi...  10.1 us
    pallas_call x1, Pallas kernels, side_pieces(): pl.pallas_call(functools.partial(side_kernel, slots, by_owner), grid=(mem...  8.35 us
    pallas_call x1, Pallas kernels, last_pieces(): pl.pallas_call(last_kernel, grid=(members,), in_specs=[SMEM, whole((heads...  6.57 us
    all_to_all x4, waiting for transfers between devices, swap(): lax.all_to_all(x, 'seq', split_axis=0, concat_axis=0, axis_index_groups=g...  5.85 us
    ppermute x1, waiting for transfers between devices, on_device(): coming = lax.ppermute(leaving, 'seq', onward)  4.75 us
    ppermute x1, starting transfers between devices, on_device(): coming = lax.ppermute(leaving, 'seq', onward)  4.47 us
  transfers between devices with their start and end apart: 5, of which 3 were waited for; matrix products, arithmetic and copies ran while one was open for 1% of the time, Pallas kernels for 44%

profile of v3, /device:TPU:0, one launch (start us, length us, event | category | flops | bytes accessed | tf_op | source)
XLA Modules:
  0.0 93.8 jit_solution(6397796354070809706)
XLA Ops:
  0.6 0.0 copy-start.5
  0.6 0.0 copy-start.7
  0.7 0.0 copy-start.9
  0.7 6.6 %last_pieces.1 = (bf16[4,528,128]{2,1,0:T(8,128)(2,1)}, f32[16,1024]{1,0:T(8,128)S(1)}) custom-call(s32[8]{0:T(128)} %len_ref.13, f32[16,1024]{1,0:T(8,128)} %bitcast.10, bf16[1024,2048]{1,0:T(8,128)(2,1)} %k_ref.7, bf16[1024,2048]{1,0:T(8,128)(2,1)} %v_ref.7), custom_call_target="tpu_custom_call" | custom-call | flops 536870912 | bytes 8388608 | tf_op jit(solution)/shard_map/last_pieces/pallas_call | solution.py:127
  7.2 5.2 %all-to-all-start.1 = ((bf16[4,528,128]{2,1,0:T(8,128)(2,1)}), bf16[4,528,128]{2,1,0:T(8,128)(2,1)S(1)}, u32[]{:S(2)}, u32[]{:S(2)}) async-start(bf16[4,528,128]{2,1,0:T(8,128)(2,1)} %get-tuple-element.39), calls=%async_computation.1 | async-start | bytes 1081344 | tf_op jit(solution)/shard_map/all_to_all | solution.py:538
  12.5 0.0 copy-done.5
  12.5 0.0 copy-done.7
  12.5 0.0 copy-done.9
  12.5 8.3 %side_pieces.3 = (bf16[4,1536,128]{2,1,0:T(8,128)(2,1)}, f32[1024,16]{1,0:T(8,128)}, s32[4]{0:T(128)S(1)}) custom-call(s32[8]{0:T(128)S(1)} %copy-done.7, s32[8]{0:T(128)S(1)} %copy-done.9, f32[16,1024]{1,0:T(8,128)S(1)} %bitcast.11, f32[16,1024]{1,0:T(8,128)S(1)} %get-tuple-element.43.crow_ref, bf16[1024,2048]{1,0:T(8,128)(2,1)} %k_ref.7, ...), custom_call_target="tpu_custom_call" | custom-call | flops 1610612736 | bytes 8388608 | tf_op jit(solution)/shard_map/side_pieces/pallas_call | solution.py:224
  20.8 0.7 fusion
  22.1 0.0 all-to-all-done.1.last_ref
  22.2 0.0 copy-start
  22.2 0.7 broadcast_in_dim.3.in_ref
  22.9 0.1 copy-done
  23.0 1.9 %leave_quad.1 = bf16[4,128,128]{2,1,0:T(8,128)(2,1)} custom-call(s32[8]{0:T(128)S(1)} %copy-done.7, bf16[4,528,128]{2,1,0:T(8,128)(2,1)} %copy-done, bf16[4,128,128]{2,1,0:T(8,128)(2,1)} %broadcast_in_dim.3.in_ref), custom_call_target="tpu_custom_call" | custom-call | tf_op jit(solution)/shard_map/leave_quad/pallas_call | solution.py:358
  25.0 0.0 copy-start.6
  25.0 0.1 conditional.1
  25.0 0.1 broadcast.3
  25.1 4.2 %all-to-all-start.3 = ((bf16[4,1536,128]{2,1,0:T(8,128)(2,1)}), bf16[4,1536,128]{2,1,0:T(8,128)(2,1)S(1)}, u32[]{:S(2)}, u32[]{:S(2)}) async-start(bf16[4,1536,128]{2,1,0:T(8,128)(2,1)} %get-tuple-element.47), calls=%async_computation.3 | async-start | bytes 3145728 | tf_op jit(solution)/shard_map/all_to_all | solution.py:538
  29.3 0.0 copy-done.6
  29.3 4.5 %collective-permute-start = (bf16[4,128,128]{2,1,0:T(8,128)(2,1)S(1)}, bf16[4,128,128]{2,1,0:T(8,128)(2,1)S(1)}, u32[]{:S(2)}, u32[]{:S(2)}) collective-permute-start(bf16[4,128,128]{2,1,0:T(8,128)(2,1)S(1)} %copy-done.6), channel_id=1, source_target_pairs={{0,8},{2,10},{4,12},{6,14},{1,9},{3,11},{5,13},{7,15},{16,24},{18,... | collective-permute-start | bytes 393224 | tf_op jit(solution)/shard_map/ppermute | solution.py:559
  33.8 10.1 %early_attention.1.local_ref = f32[1024,768]{1,0:T(8,128)} custom-call(s32[8]{0:T(128)S(1)} %copy-done.7, bf16[1024,2048]{1,0:T(8,128)(2,1)} %q_ref.3, bf16[1024,2048]{1,0:T(8,128)(2,1)} %k_ref.7, bf16[1024,2048]{1,0:T(8,128)(2,1)} %v_ref.7, f32[16,1024]{1,0:T(8,128)S(1)} %get-tuple-element.43.crow_ref, f32[1024,16]{1,0:T(8,128)} %get-tuple-element.44.ccol_ref), custom_call_target="tpu_custom_call" | custom-call | flops 1610612736 | bytes 7864320 | tf_op jit(solution)/shard_map/early_attention/pallas_call | solution.py:314
  43.8 0.0 copy-start.8
  43.8 4.7 %collective-permute-done.in_ref = bf16[4,128,128]{2,1,0:T(8,128)(2,1)S(1)} collective-permute-done((bf16[4,128,128]{2,1,0:T(8,128)(2,1)S(1)}, bf16[4,128,128]{2,1,0:T(8,128)(2,1)S(1)}, u32[]{:S(2)}, u32[]{:S(2)}) %collective-permute-start) | collective-permute-done | bytes 131104 | tf_op jit(solution)/shard_map/ppermute | solution.py:559
  48.6 0.0 copy-start.4
  48.6 0.7 copy-done.4
  49.2 2.0 %enter_states.1 = bf16[4,4,128,128]{3,2,1,0:T(8,128)(2,1)} custom-call(s32[8]{0:T(128)S(1)} %copy-done.7, bf16[4,528,128]{2,1,0:T(8,128)(2,1)} %copy-done, bf16[4,128,128]{2,1,0:T(8,128)(2,1)} %copy-done.4), custom_call_target="tpu_custom_call" | custom-call | tf_op jit(solution)/shard_map/enter_states/pallas_call | solution.py:379
  51.3 0.0 all-to-all-done.3.side_ref
  51.3 0.0 copy-start.1
  51.3 3.5 %all-to-all-start.2 = ((bf16[4,4,128,128]{3,2,1,0:T(8,128)(2,1)}), bf16[4,4,128,128]{3,2,1,0:T(8,128)(2,1)S(1)}, u32[]{:S(2)}, u32[]{:S(2)}) async-start(bf16[4,4,128,128]{3,2,1,0:T(8,128)(2,1)} %enter_states.1), calls=%async_computation.2 | async-start | bytes 1048576 | tf_op jit(solution)/shard_map/all_to_all | solution.py:538
  54.7 0.0 copy-done.1
  54.7 3.1 %final_states.1 = bf16[8,4,128,128]{3,2,1,0:T(8,128)(2,1)} custom-call(s32[8]{0:T(128)S(1)} %copy-done.7, s32[8]{0:T(128)S(1)} %copy-done.9, bf16[4,528,128]{2,1,0:T(8,128)(2,1)} %copy-done, bf16[4,1536,128]{2,1,0:T(8,128)(2,1)} %copy-done.1, bf16[4,128,128]{2,1,0:T(8,128)(2,1)} %copy-done.4), custom_call_target="tpu_custom_call" | custom-call | tf_op jit(solution)/shard_map/final_states/pallas_call | solution.py:428
  57.9 3.7 %all-to-all-done.2 = bf16[4,4,128,128]{3,2,1,0:T(8,128)(2,1)S(1)} async-done(((bf16[4,4,128,128]{3,2,1,0:T(8,128)(2,1)}), bf16[4,4,128,128]{3,2,1,0:T(8,128)(2,1)S(1)}, u32[]{:S(2)}, u32[]{:S(2)}) %all-to-all-start.2) | async-done | bytes 524320 | tf_op jit(solution)/shard_map/all_to_all | solution.py:538
  61.5 0.0 copy-start.3
  61.6 5.3 %all-to-all-start.4 = ((bf16[8,4,128,128]{3,2,1,0:T(8,128)(2,1)}), bf16[8,4,128,128]{3,2,1,0:T(8,128)(2,1)S(1)}, u32[]{:S(2)}, u32[]{:S(2)}) async-start(bf16[8,4,128,128]{3,2,1,0:T(8,128)(2,1)} %final_states.1), calls=%async_computation.4 | async-start | bytes 2097152 | tf_op jit(solution)/shard_map/all_to_all | solution.py:538
  69.4 0.0 copy-done.8
  69.4 0.6 reshape.21.gain_ref
  70.0 0.0 copy-done.3
  70.1 18.0 %finish.1 = bf16[1024,2048]{1,0:T(8,128)(2,1)} custom-call(s32[8]{0:T(128)S(1)} %copy-done.7, bf16[1024,2048]{1,0:T(8,128)(2,1)} %q_ref.3, bf16[1024,2048]{1,0:T(8,128)(2,1)} %k_ref.7, bf16[1024,2048]{1,0:T(8,128)(2,1)} %v_ref.7, bf16[16,128,128]{2,1,0:T(8,128)(2,1)} %bitcast.9, f32[1024,768]{1,0:T(8,128)} %early_attention.1.local_ref, ...), custom_call_target="tpu_custom_call" | custom-call | flops 4294967296 | bytes 20971520 | tf_op jit(solution)/shard_map/finish/pallas_call | solution.py:486
  88.0 2.2 %all-to-all-done.4 = bf16[8,4,128,128]{3,2,1,0:T(8,128)(2,1)S(1)} async-done(((bf16[8,4,128,128]{3,2,1,0:T(8,128)(2,1)}), bf16[8,4,128,128]{3,2,1,0:T(8,128)(2,1)S(1)}, u32[]{:S(2)}, u32[]{:S(2)}) %all-to-all-start.4) | async-done | bytes 1048608 | tf_op jit(solution)/shard_map/all_to_all | solution.py:538
  90.2 0.0 copy-start.2
  90.2 1.0 %copy-done.2 = bf16[8,4,128,128]{3,2,1,0:T(8,128)(2,1)} copy-done((bf16[8,4,128,128]{3,2,1,0:T(8,128)(2,1)}, bf16[8,4,128,128]{3,2,1,0:T(8,128)(2,1)S(1)}, u32[]{:S(2)}) %copy-start.2) | copy-done | bytes 1048600
  91.2 2.5 %pick_owned.1 = bf16[1,16,128,128]{3,2,1,0:T(8,128)(2,1)} custom-call(s32[1]{0:T(128)} %bitcast.5.quad_ref, s32[1]{0:T(128)} %get-tuple-element.51.late_ref, bf16[2,16,128,128]{3,2,1,0:T(8,128)(2,1)} %bitcast.8, bf16[1,16,128,128]{3,2,1,0:T(8,128)(2,1)S(1)} %get-tuple-element.54.rest_ref), custom_call_target="tpu_custom_call" | custom-call | tf_op jit(solution)/shard_map/pick_owned/pallas_call | solution.py:523
Async XLA Ops:
  0.6 11.9 %copy-start.5 = (f32[1024,16]{0,1:T(8,128)S(1)}, f32[1024,16]{0,1:T(8,128)}, u32[]{:S(2)}) copy-start(f32[1024,16]{0,1:T(8,128)} %param.13) | copy-start | bytes 196612
  0.6 11.8 %copy-start.7 = (s32[8]{0:T(128)S(1)}, s32[8]{0:T(128)}, u32[]{:S(2)}) copy-start(s32[8]{0:T(128)} %len_ref.13) | copy-start | bytes 100
  0.7 11.8 %copy-start.9 = (s32[8]{0:T(128)S(1)}, s32[8]{0:T(128)}, u32[]{:S(2)}) copy-start(s32[8]{0:T(128)} %own_ref.3) | copy-start | bytes 100
  7.2 14.9 %all-to-all-start.1 = ((bf16[4,528,128]{2,1,0:T(8,128)(2,1)}), bf16[4,528,128]{2,1,0:T(8,128)(2,1)S(1)}, u32[]{:S(2)}, u32[]{:S(2)}) async-start(bf16[4,528,128]{2,1,0:T(8,128)(2,1)} %get-tuple-element.39), calls=%async_computation.1 | async-start | bytes 1081344 | tf_op jit(solution)/shard_map/all_to_all | solution.py:538
  22.2 0.9 copy-start
  25.0 4.3 %copy-start.6 = (bf16[4,128,128]{2,1,0:T(8,128)(2,1)S(1)}, bf16[4,128,128]{2,1,0:T(8,128)(2,1)}, u32[]{:S(2)}) copy-start(bf16[4,128,128]{2,1,0:T(8,128)(2,1)} %leave_quad.1) | copy-start | bytes 393220
  25.1 26.2 %all-to-all-start.3 = ((bf16[4,1536,128]{2,1,0:T(8,128)(2,1)}), bf16[4,1536,128]{2,1,0:T(8,128)(2,1)S(1)}, u32[]{:S(2)}, u32[]{:S(2)}) async-start(bf16[4,1536,128]{2,1,0:T(8,128)(2,1)} %get-tuple-element.47), calls=%async_computation.3 | async-start | bytes 3145728 | tf_op jit(solution)/shard_map/all_to_all | solution.py:538
  29.3 19.3 %collective-permute-start = (bf16[4,128,128]{2,1,0:T(8,128)(2,1)S(1)}, bf16[4,128,128]{2,1,0:T(8,128)(2,1)S(1)}, u32[]{:S(2)}, u32[]{:S(2)}) collective-permute-start(bf16[4,128,128]{2,1,0:T(8,128)(2,1)S(1)} %copy-done.6), channel_id=1, source_target_pairs={{0,8},{2,10},{4,12},{6,14},{1,9},{3,11},{5,13},{7,15},{16,24},{18,... | collective-permute-start | bytes 393224 | tf_op jit(solution)/shard_map/ppermute | solution.py:559
  43.8 25.6 %copy-start.8 = (bf16[2048]{0:T(1024)(128)(2,1)S(1)}, bf16[2048]{0:T(1024)(128)(2,1)}, u32[]{:S(2)}) copy-start(bf16[2048]{0:T(1024)(128)(2,1)} %param.15) | copy-start | bytes 12292
  48.6 0.7 copy-start.4
  51.3 3.5 %copy-start.1 = (bf16[4,1536,128]{2,1,0:T(8,128)(2,1)}, bf16[4,1536,128]{2,1,0:T(8,128)(2,1)S(1)}, u32[]{:S(2)}) copy-start(bf16[4,1536,128]{2,1,0:T(8,128)(2,1)S(1)} %all-to-all-done.3.side_ref) | copy-start | bytes 4718596
  51.3 10.3 %all-to-all-start.2 = ((bf16[4,4,128,128]{3,2,1,0:T(8,128)(2,1)}), bf16[4,4,128,128]{3,2,1,0:T(8,128)(2,1)S(1)}, u32[]{:S(2)}, u32[]{:S(2)}) async-start(bf16[4,4,128,128]{3,2,1,0:T(8,128)(2,1)} %enter_states.1), calls=%async_computation.2 | async-start | bytes 1048576 | tf_op jit(solution)/shard_map/all_to_all | solution.py:538
  61.5 8.5 %copy-start.3 = (bf16[4,4,128,128]{3,2,1,0:T(8,128)(2,1)}, bf16[4,4,128,128]{3,2,1,0:T(8,128)(2,1)S(1)}, u32[]{:S(2)}) copy-start(bf16[4,4,128,128]{3,2,1,0:T(8,128)(2,1)S(1)} %all-to-all-done.2) | copy-start | bytes 1572868
  61.6 28.7 %all-to-all-start.4 = ((bf16[8,4,128,128]{3,2,1,0:T(8,128)(2,1)}), bf16[8,4,128,128]{3,2,1,0:T(8,128)(2,1)S(1)}, u32[]{:S(2)}, u32[]{:S(2)}) async-start(bf16[8,4,128,128]{3,2,1,0:T(8,128)(2,1)} %final_states.1), calls=%async_computation.4 | async-start | bytes 2097152 | tf_op jit(solution)/shard_map/all_to_all | solution.py:538
  90.2 1.0 %copy-start.2 = (bf16[8,4,128,128]{3,2,1,0:T(8,128)(2,1)}, bf16[8,4,128,128]{3,2,1,0:T(8,128)(2,1)S(1)}, u32[]{:S(2)}) copy-start(bf16[8,4,128,128]{3,2,1,0:T(8,128)(2,1)S(1)} %all-to-all-done.4) | copy-start | bytes 3145732

commit v4 on v3

--- a/solution.py
+++ b/solution.py
@@ -11,8 +11,9 @@
 BLK = 512
 SIDE = 3
 EXTRA = 16
-CHUNK = 256
-EARLY = 6
+CHUNK = 128
+MEMBERS = 4
+EARLY = 4
 NEG = -1e30
 LOG2E = math.log2(math.e)
 SCALE = 128**-0.5
@@ -20,6 +21,7 @@
 SMEM = pl.BlockSpec(memory_space=pltpu.SMEM)
 VMEM = pl.BlockSpec(memory_space=pltpu.VMEM)
 LIMIT = pltpu.CompilerParams(vmem_limit_bytes=60 * 2**20)
+SMALL = pltpu.CompilerParams(vmem_limit_bytes=48 * 2**20)
 
 
 def dot(a, b, contract=((1,), (0,))):
@@ -80,13 +82,12 @@
     return jnp.exp2(jnp.where(inside, value_at(cum, at, high) - cum, NEG) + math.log2(SCALE))
 
 
-def weigh(keys, w_ref, h):
-    flipped = keys.T.astype(F32)
-    weights = [jnp.broadcast_to(w_ref[pl.ds(h + j, 1), :], (128, keys.shape[0])) for j in range(2)]
-    return (flipped * jnp.concatenate(weights, axis=0)).astype(BF16)
-
-
-def last_kernel(len_ref, ld_ref, k_ref, v_ref, out_ref, crow_ref, w_ref, first_ref):
+def weigh(flipped, w_ref, h):
+    weights = [jnp.broadcast_to(w_ref[pl.ds(h + j, 1), :], (128, flipped.shape[1])) for j in range(2)]
+    return (flipped.astype(F32) * jnp.concatenate(weights, axis=0)).astype(BF16)
+
+
+def last_kernel(len_ref, ld_ref, k_ref, v_ref, out_ref, crow_ref, kt_ref, w_ref, first_ref):
     heads, rows = ld_ref.shape
     step = pl.program_id(0)
     hp = k_ref.shape[1] // 128
@@ -106,7 +107,9 @@
 
     for i in range(0, hp, 2):
         lanes = slice(i * 128, (i + 2) * 128)
-        states = dot(weigh(k_ref[:, lanes], w_ref, step * hp + i), v_ref[:, lanes])
+        flipped = k_ref[:, lanes].T
+        kt_ref[lanes, :] = flipped
+        states = dot(weigh(flipped, w_ref, step * hp + i), v_ref[:, lanes])
         out_ref[0, i * 128 : (i + 1) * 128, :] = states[:128, :128].astype(BF16)
         out_ref[0, (i + 1) * 128 : (i + 2) * 128, :] = states[128:, 128:].astype(BF16)
     rate = first_ref[pl.ds(step * hp, hp), :]
@@ -128,24 +131,29 @@
         last_kernel,
         grid=(members,),
         in_specs=[SMEM, whole((heads, rows)), wide, wide],
-        out_specs=[pl.BlockSpec((1, size, 128), lambda j: (j, 0, 0)), whole((heads, rows))],
+        out_specs=[
+            pl.BlockSpec((1, size, 128), lambda j: (j, 0, 0)),
+            whole((heads, rows)),
+            pl.BlockSpec((hp * 128, rows), lambda j: (j, 0)),
+        ],
         out_shape=[
             jax.ShapeDtypeStruct((members, size, 128), BF16),
             jax.ShapeDtypeStruct((heads, rows), F32),
+            jax.ShapeDtypeStruct((heads * 128, rows), BF16),
         ],
         scratch_shapes=[pltpu.VMEM((heads, rows), F32), pltpu.VMEM((heads, 128), F32)],
         compiler_params=LIMIT,
         cost_estimate=pl.CostEstimate(
-            flops=heads * rows * 128 * 256, bytes_accessed=rows * heads * 128 * 4, transcendentals=heads * rows
+            flops=heads * rows * 128 * 256, bytes_accessed=rows * heads * 128 * 6, transcendentals=heads * rows
         ),
         name="last_pieces",
     )(doc_lengths, decay_rows, keys, values)
 
 
-def side_kernel(slots, by_owner, len_ref, own_ref, ld_ref, crow_ref, k_ref, v_ref, out_ref, ccol_ref, flag_ref, w_ref, keep_ref):
+def side_kernel(slots, by_owner, len_ref, own_ref, ld_ref, crow_ref, kt_ref, v_ref, out_ref, ccol_ref, flag_ref, w_ref, keep_ref):
     heads, rows = crow_ref.shape
     step = pl.program_id(0)
-    hp = k_ref.shape[1] // 128
+    hp = v_ref.shape[1] // 128
 
     @pl.when(step == 0)
     def _():
@@ -183,9 +191,10 @@
             crowded = jnp.maximum(crowded, late)
             owned_in = jnp.where(own_ref[d] == me, device, owned_in)
             owned_late = jnp.where(own_ref[d] == me, late, owned_late)
-        flag_ref[0] = owned_in
+        flag_ref[0] = owned_in // MEMBERS
         flag_ref[1] = owned_late
         flag_ref[2] = crowded
+        flag_ref[3] = owned_in
         at = iota((heads, rows), 1)
         cum = crow_ref[...]
         row_at = iota((16, rows), 1)
@@ -198,7 +207,7 @@
 
     for i in range(0, hp, 2):
         lanes = slice(i * 128, (i + 2) * 128)
-        weighted = weigh(k_ref[:, lanes], w_ref, step * hp + i).reshape(16, 16, rows)
+        weighted = weigh(kt_ref[lanes, :], w_ref, step * hp + i).reshape(16, 16, rows)
         for s in range(slots):
             kept = (weighted * keep_ref[s][None]).reshape(256, rows)
             states = dot(kept, v_ref[:, lanes])
@@ -211,7 +220,7 @@
                     out_ref[0, at : at + 128, :] = state
 
 
-def side_pieces(doc_lengths, owner_ids, decay_rows, crow, keys, values, members, slots, by_owner):
+def side_pieces(doc_lengths, owner_ids, decay_rows, crow, flipped, values, members, slots, by_owner):
     heads, rows = crow.shape
     hp = heads // members
     wide = pl.BlockSpec((rows, hp * 128), lambda j: (0, j))
@@ -224,7 +233,14 @@
     return pl.pallas_call(
         functools.partial(side_kernel, slots, by_owner),
         grid=(members,),
-        in_specs=[SMEM, SMEM, whole((heads, rows)), whole((heads, rows)), wide, wide],
+        in_specs=[
+            SMEM,
+            SMEM,
+            whole((heads, rows)),
+            whole((heads, rows)),
+            pl.BlockSpec((hp * 128, rows), lambda j: (j, 0)),
+            wide,
+        ],
         out_specs=[out_spec, whole((rows, heads)), SMEM],
         out_shape=[out, jax.ShapeDtypeStruct((rows, heads), F32), jax.ShapeDtypeStruct((4,), jnp.int32)],
         scratch_shapes=[pltpu.VMEM((heads, rows), F32), pltpu.VMEM((slots, 16, rows), BF16)],
@@ -233,7 +249,7 @@
             flops=slots * heads * rows * 128 * 256, bytes_accessed=rows * heads * 128 * 4, transcendentals=heads * rows
         ),
         name="side_pieces",
-    )(doc_lengths, owner_ids, decay_rows, crow, keys, values)
+    )(doc_lengths, owner_ids, decay_rows, crow, flipped, values)
 
 
 def head_column(ccol_ref, h):
@@ -251,42 +267,34 @@
         bias_ref[c * CHUNK : (c + 1) * CHUNK, :] = jnp.where(keep, math.log2(SCALE), NEG)
 
 
-def attend(first, ends, q_ref, k_ref, v_ref, lanes, row_all, col_all, bias_ref, state, emit):
+def attend(first, ends, q_ref, kt_ref, v_ref, lanes, row_all, col_all, bias_ref, state, emit):
     rows = q_ref.shape[0]
-    half = CHUNK // 2
-    for c in range(rows // CHUNK):
-        r0 = c * CHUNK
-        key = k_ref[r0 : r0 + CHUNK, lanes]
-        value = v_ref[r0 : r0 + CHUNK, lanes]
-        row = row_all[:, r0 : r0 + CHUNK]
-        base = row_all[:, r0 - 1 : r0] if c else jnp.zeros((1, 1), F32)
+    for r0 in range(0, rows, CHUNK):
+        span = slice(r0, r0 + CHUNK)
+        query, flipped, value = q_ref[span, lanes], kt_ref[lanes, span], v_ref[span, lanes]
+        row, col = row_all[:, span], col_all[span]
+        base = row_all[:, r0 - 1 : r0] if r0 else jnp.zeros((1, 1), F32)
         reach = run_end(ends, first + r0 - 1) - (first + r0)
-        state_bf = None if state is None else state.astype(BF16)
-        for part in range(2):
-            t0 = r0 + part * half
-            width = (part + 1) * half
-            query = q_ref[t0 : t0 + half, lanes]
-            col = col_all[t0 : t0 + half]
-            scores = dot(query, key[:width], ((1,), (1,)))
-            decay = jnp.exp2((col - row[:, :width]) + bias_ref[t0 : t0 + half, :width])
-            att = dot((scores * decay).astype(BF16), value[:width])
-            if state is not None:
-                at = part * half + iota((half, 1), 0)
-                lead = jnp.exp2(jnp.where(at < reach, col - base, NEG))
-                att = att + lead * dot(query, state_bf)
-            emit(t0, half, att)
+        decay = jnp.exp2((col - row) + bias_ref[span, :])
+        if state is None:
+            att = dot((dot(query, flipped) * decay).astype(BF16), value)
+        else:
+            both = dot(query, jnp.concatenate([flipped, state.astype(BF16)], axis=1))
+            lead = jnp.exp2(jnp.where(iota((CHUNK, 1), 0) < reach, col - base, NEG))
+            att = dot((both[:, :CHUNK] * decay).astype(BF16), value) + lead * both[:, CHUNK:]
+        emit(r0, CHUNK, att)
         if r0 + CHUNK < rows:
             since = run_start(ends, first + r0 + CHUNK - 1) - (first + r0)
             total = row[:, CHUNK - 1 :]
             inside = iota((1, CHUNK), 1) >= since
             weight = jnp.exp2(jnp.where(inside, total - row, NEG) + math.log2(SCALE))
-            fresh = dot((key.T.astype(F32) * weight).astype(BF16), value)
+            fresh = dot((flipped.astype(F32) * weight).astype(BF16), value)
             if state is not None:
                 fresh = fresh + state * jnp.exp2(jnp.where(CHUNK <= reach, total - base, NEG))
             state = fresh
 
 
-def early_kernel(len_ref, q_ref, k_ref, v_ref, crow_ref, ccol_ref, out_ref, bias_ref):
+def early_kernel(pairs_before, len_ref, q_ref, kt_ref, v_ref, crow_ref, ccol_ref, out_ref, bias_ref):
     rows = q_ref.shape[0]
     step = pl.program_id(0)
     first = lax.axis_index("seq") * rows
@@ -297,25 +305,32 @@
         fill_bias(first, ends, bias_ref)
 
     for i in range(2):
-        h = step * 2 + i
+        h = (step + pairs_before) * 2 + i
         lanes = slice(i * 128, (i + 1) * 128)
 
         def emit(t0, size, att):
             out_ref[t0 : t0 + size, lanes] = att
 
-        attend(
-            first, ends, q_ref, k_ref, v_ref, lanes, crow_ref[pl.ds(h, 1), :], head_column(ccol_ref, h), bias_ref, None, emit
-        )
-
-
-def early_attention(doc_lengths, queries, keys, values, crow, ccol):
+        row_all, col_all = crow_ref[pl.ds(h, 1), :], head_column(ccol_ref, h)
+        attend(first, ends, q_ref, kt_ref, v_ref, lanes, row_all, col_all, bias_ref, None, emit)
+
+
+def early_attention(doc_lengths, queries, flipped, values, crow, ccol, heads_before):
     heads, rows = crow.shape
-    wide = pl.BlockSpec((rows, 256), lambda j: (0, j))
+    skip = heads_before // 2
+    wide = pl.BlockSpec((rows, 256), lambda j: (0, j + skip))
     return pl.pallas_call(
-        early_kernel,
+        functools.partial(early_kernel, skip),
         grid=(EARLY // 2,),
-        in_specs=[SMEM, wide, wide, wide, whole((heads, rows)), whole((rows, heads))],
-        out_specs=wide,
+        in_specs=[
+            SMEM,
+            wide,
+            pl.BlockSpec((256, rows), lambda j: (j + skip, 0)),
+            wide,
+            whole((heads, rows)),
+            whole((rows, heads)),
+        ],
+        out_specs=pl.BlockSpec((rows, 256), lambda j: (0, j)),
         out_shape=jax.ShapeDtypeStruct((rows, EARLY * 128), F32),
         scratch_shapes=[pltpu.VMEM((rows, CHUNK), F32)],
         compiler_params=LIMIT,
@@ -323,7 +338,7 @@
             flops=EARLY * rows * CHUNK * 128 * 8, bytes_accessed=rows * EARLY * 128 * 10, transcendentals=EARLY * rows * CHUNK
         ),
         name="early_attention",
-    )(doc_lengths, queries, keys, values, crow, ccol)
+    )(doc_lengths, queries, flipped, values, crow, ccol)
 
 
 def decay_of(last_ref, e, i, hp):
@@ -347,41 +362,49 @@
     return state
 
 
-def leave_kernel(rows, len_ref, last_ref, in_ref, out_ref):
-    hp = in_ref.shape[0]
+def leave_kernel(rows, len_ref, last_ref, *refs):
+    out_ref = refs[-1]
+    hp = out_ref.shape[0]
     for i in range(hp):
-        state = scan_quad(rows, len_ref, last_ref, in_ref[i].astype(F32), i, hp, lambda e, x: None)
+        state = refs[0][i].astype(F32) if len(refs) > 1 else jnp.zeros((128, 128), F32)
+        state = scan_quad(rows, len_ref, last_ref, state, i, hp, lambda e, x: None)
         out_ref[i] = state.astype(BF16)
 
 
-def leave_quad(doc_lengths, last, coming, rows):
+def leave_quad(doc_lengths, last, coming, rows, hp):
     return pl.pallas_call(
         functools.partial(leave_kernel, rows),
-        in_specs=[SMEM, VMEM, VMEM],
+        in_specs=[SMEM] + [VMEM] * (1 + len(coming)),
         out_specs=VMEM,
-        out_shape=jax.ShapeDtypeStruct(coming.shape, BF16),
-        compiler_params=LIMIT,
+        out_shape=jax.ShapeDtypeStruct((hp, 128, 128), BF16),
+        compiler_params=SMALL,
         name="leave_quad",
-    )(doc_lengths, last, coming)
-
-
-def enter_kernel(rows, len_ref, last_ref, in_ref, out_ref):
+    )(doc_lengths, last, *coming)
+
+
+def enter_kernel(rows, len_ref, last_ref, in_ref, *refs):
+    out_refs, state_ref = refs[:-1], refs[-1]
     hp = in_ref.shape[0]
 
     def note(i, e, state):
-        out_ref[e, i] = state.astype(BF16)
+        state_ref[e, i] = state
 
     for i in range(hp):
         scan_quad(rows, len_ref, last_ref, in_ref[i].astype(F32), i, hp, functools.partial(note, i))
+    me = lax.axis_index("seq") % len(out_refs)
+    for x, out_ref in enumerate(out_refs):
+        out_ref[...] = state_ref[me ^ x].astype(BF16)
 
 
 def enter_states(doc_lengths, last, coming, rows):
+    members = last.shape[0]
     return pl.pallas_call(
         functools.partial(enter_kernel, rows),
         in_specs=[SMEM, VMEM, VMEM],
-        out_specs=VMEM,
-        out_shape=jax.ShapeDtypeStruct((last.shape[0],) + coming.shape, BF16),
-        compiler_params=LIMIT,
+        out_specs=[VMEM] * members,
+        out_shape=[jax.ShapeDtypeStruct(coming.shape, BF16)] * members,
+        scratch_shapes=[pltpu.VMEM((members,) + coming.shape, F32)],
+        compiler_params=SMALL,
         name="enter_states",
     )(doc_lengths, last, coming)
 
@@ -431,68 +454,87 @@
         out_specs=VMEM,
         out_shape=jax.ShapeDtypeStruct((spread,) + coming.shape, BF16),
         scratch_shapes=[pltpu.VMEM((last.shape[0],) + coming.shape, F32)],
-        compiler_params=LIMIT,
+        compiler_params=SMALL,
         name="final_states",
     )(doc_lengths, owner_ids, last, side, coming)
 
 
 def finish_kernel(
-    len_ref, q_ref, k_ref, v_ref, enter_ref, local_ref, gate_ref, gain_ref, crow_ref, ccol_ref, out_ref, bias_ref
+    len_ref, q_ref, kt_ref, v_ref, e0, e1, e2, e3, local1_ref, local2_ref, gate_ref, gain_ref, crow_ref, ccol_ref, out_ref, bias_ref
 ):
     rows = q_ref.shape[0]
     step = pl.program_id(0)
-    first = lax.axis_index("seq") * rows
+    me = lax.axis_index("seq")
+    first = me * rows
     ends = read_ends(len_ref, len_ref.shape[0])
+    hp = e0.shape[0]
+
+    def entering(h):
+        far = (h // hp) ^ (me % MEMBERS)
+        state = e0[h % hp]
+        for x, ref in ((1, e1), (2, e2), (3, e3)):
+            state = jnp.where(far == x, ref[h % hp], state)
+        return state
 
     def emit(lanes, t0, size, att):
         mean = jnp.mean(att * att, axis=1, keepdims=True)
-        gate = 1.0 / (1.0 + jnp.exp(-gate_ref[t0 : t0 + size, lanes].astype(F32)))
+        gate = 0.5 + 0.5 * jnp.tanh(0.5 * gate_ref[t0 : t0 + size, lanes].astype(F32))
         gain = gain_ref[:, lanes].astype(F32)
-        out_ref[t0 : t0 + size, lanes] = (att * lax.rsqrt(mean + 1e-06) * gain * gate).astype(BF16)
-
-    @pl.when(step == 0)
-    def _():
-        fill_bias(first, ends, bias_ref)
-
-    @pl.when(step < EARLY // 2)
-    def _():
+        out_ref[t0 : t0 + size, lanes] = (att * lax.rsqrt(mean + 1e-06) * (gain * gate)).astype(BF16)
+
+    def add_carry(local_ref):
         reach = run_end(ends, first - 1) - first
         for i in range(2):
             lanes = slice(i * 128, (i + 1) * 128)
             col_all = head_column(ccol_ref, step * 2 + i)
-            for t0 in range(0, rows, CHUNK):
-                at = t0 + iota((CHUNK, 1), 0)
-                lead = jnp.exp2(jnp.where(at < reach, col_all[t0 : t0 + CHUNK], NEG))
-                carry = dot(q_ref[t0 : t0 + CHUNK, lanes], enter_ref[i])
-                emit(lanes, t0, CHUNK, local_ref[t0 : t0 + CHUNK, lanes] + lead * carry)
-
-    @pl.when(step >= EARLY // 2)
+            state = entering(step * 2 + i)
+            for t0 in range(0, rows, 256):
+                at = t0 + iota((256, 1), 0)
+                lead = jnp.exp2(jnp.where(at < reach, col_all[t0 : t0 + 256], NEG))
+                carry = dot(q_ref[t0 : t0 + 256, lanes], state)
+                emit(lanes, t0, 256, local_ref[t0 : t0 + 256, lanes] + lead * carry)
+
+    @pl.when(step == 0)
+    def _():
+        fill_bias(first, ends, bias_ref)
+
+    @pl.when(step < EARLY // 2)
+    def _():
+        add_carry(local1_ref)
+
+    @pl.when((step >= EARLY // 2) & (step < EARLY))
+    def _():
+        add_carry(local2_ref)
+
+    @pl.when(step >= EARLY)
     def _():
         for i in range(2):
             h = step * 2 + i
             lanes = slice(i * 128, (i + 1) * 128)
             row_all, col_all = crow_ref[pl.ds(h, 1), :], head_column(ccol_ref, h)
-            state = enter_ref[i].astype(F32)
+            state = entering(h).astype(F32)
             attend(
-                first, ends, q_ref, k_ref, v_ref, lanes, row_all, col_all, bias_ref, state, functools.partial(emit, lanes)
+                first, ends, q_ref, kt_ref, v_ref, lanes, row_all, col_all, bias_ref, state, functools.partial(emit, lanes)
             )
 
 
-def finish(doc_lengths, queries, keys, values, entering, local, gate, gain, crow, ccol):
+def finish(doc_lengths, queries, flipped, values, entering, local1, local2, gate, gain, crow, ccol):
     heads, rows = crow.shape
     pairs = EARLY // 2
     wide = pl.BlockSpec((rows, 256), lambda j: (0, j))
-    late = pl.BlockSpec((rows, 256), lambda j: (0, jnp.maximum(j, pairs)))
     return pl.pallas_call(
         finish_kernel,
         grid=(heads // 2,),
         in_specs=[
             SMEM,
             wide,
-            late,
-            late,
-            pl.BlockSpec((2, 128, 128), lambda j: (j, 0, 0)),
+            pl.BlockSpec((256, rows), lambda j: (jnp.maximum(j, EARLY), 0)),
+            pl.BlockSpec((rows, 256), lambda j: (0, jnp.maximum(j, EARLY))),
+        ]
+        + [whole(e.shape) for e in entering]
+        + [
             pl.BlockSpec((rows, 256), lambda j: (0, jnp.minimum(j, pairs - 1))),
+            pl.BlockSpec((rows, 256), lambda j: (0, jnp.clip(j - pairs, 0, pairs - 1))),
             wide,
             pl.BlockSpec((1, 256), lambda j: (0, j)),
             whole((heads, rows)),
@@ -506,32 +548,7 @@
             flops=heads * rows * CHUNK * 128 * 8, bytes_accessed=rows * heads * 128 * 10, transcendentals=heads * rows * CHUNK
         ),
         name="finish",
-    )(doc_lengths, queries, keys, values, entering, local, gate, gain.reshape(1, -1), crow, ccol)
-
-
-def pick_kernel(quad_ref, late_ref, in_ref, rest_ref, out_ref):
-    out_ref[...] = in_ref[...]
-
-    @pl.when(late_ref[0] > 0)
-    def _():
-        out_ref[...] = rest_ref[...]
-
-
-def pick_owned(quad, late, arrived, rest):
-    shape = rest.shape
-    block = lambda index: pl.BlockSpec(shape, index)
-    return pl.pallas_call(
-        pick_kernel,
-        grid_spec=pltpu.PrefetchScalarGridSpec(
-            num_scalar_prefetch=2,
-            grid=(1,),
-            in_specs=[block(lambda j, quad, late: (quad[0], 0, 0, 0)), block(lambda j, quad, late: (0, 0, 0, 0))],
-            out_specs=block(lambda j, quad, late: (0, 0, 0, 0)),
-        ),
-        out_shape=jax.ShapeDtypeStruct(shape, BF16),
-        compiler_params=LIMIT,
-        name="pick_owned",
-    )(quad, late, arrived, rest)
+    )(doc_lengths, queries, flipped, values, *entering, local1, local2, gate, gain.reshape(1, -1), crow, ccol)
 
 
 def swap(x, groups=None):
@@ -540,42 +557,46 @@
 
 def on_device(spread, queries, keys, values, log_decay, gate, gain, doc_lengths, owner_ids):
     rows, heads = log_decay.shape
-    members = 4
-    quads = spread // members
-    hp = heads // members
-    near = [[q * members + m for m in range(members)] for q in range(quads)]
-    onward = [(s, s + members) for s in range(spread - members)]
+    quads = spread // MEMBERS
+    hp = heads // MEMBERS
+    near = [[q * MEMBERS + m for m in range(MEMBERS)] for q in range(quads)]
+    onward = [(s, s + MEMBERS) for s in range(spread - MEMBERS)]
     decay_rows = log_decay.T
 
-    last, crow = last_pieces(doc_lengths, decay_rows, keys, values, members)
+    last, crow, flipped = last_pieces(doc_lengths, decay_rows, keys, values, MEMBERS)
     last = swap(last, near)
-    side, ccol, flags = side_pieces(doc_lengths, owner_ids, decay_rows, crow, keys, values, members, SIDE, False)
+    side, ccol, flags = side_pieces(doc_lengths, owner_ids, decay_rows, crow, flipped, values, MEMBERS, SIDE, False)
     last, side = lax.optimization_barrier((last, side))
+
+    coming = []
+    for _ in range(quads - 1):
+        leaving = leave_quad(doc_lengths, last, coming, rows, hp)
+        coming = [lax.ppermute(leaving, "seq", onward)]
+    side, crow_1, leaving = lax.optimization_barrier((side, crow, leaving))
     side = swap(side, near)
-
-    coming = jnp.zeros((hp, 128, 128), BF16)
-    for _ in range(quads - 1):
-        leaving = leave_quad(doc_lengths, last, coming, rows)
-        coming = lax.ppermute(leaving, "seq", onward)
-    crow_after, _ = lax.optimization_barrier((crow, leaving))
-    local = early_attention(doc_lengths, queries, keys, values, crow_after, ccol)
+    local1 = early_attention(doc_lengths, queries, flipped, values, crow_1, ccol, 0)
 
     def send_rest():
         rest, _, _ = side_pieces(
-            doc_lengths, owner_ids, decay_rows, crow_after, keys, values, heads // 2, spread, True
+            doc_lengths, owner_ids, decay_rows, crow_1, flipped, values, heads // 2, spread, True
         )
-        return lax.dynamic_index_in_dim(swap(rest), flags[0], 0, True)
-
+        return lax.dynamic_index_in_dim(swap(rest), flags[3], 0, True)
+
+    coming, local1 = lax.optimization_barrier((coming[0], local1))
+    entering = enter_states(doc_lengths, last, coming, rows)
+    crow_2, entering = lax.optimization_barrier((crow_1, entering))
+    entering = [entering[0]] + [
+        lax.ppermute(entering[x], "seq", [(s, s ^ x) for s in range(spread)]) for x in range(1, MEMBERS)
+    ]
+    local2 = early_attention(doc_lengths, queries, flipped, values, crow_2, ccol, EARLY)
     rest = lax.cond(flags[2] > 0, send_rest, lambda: jnp.zeros((1, heads, 128, 128), BF16))
-    coming, local, rest = lax.optimization_barrier((coming, local, rest))
-
-    entering = swap(enter_states(doc_lengths, last, coming, rows), near).reshape(heads, 128, 128)
+    side, local2, rest = lax.optimization_barrier((side, local2, rest))
     finals = final_states(doc_lengths, owner_ids, last, side, coming, rows, spread)
     arrived = swap(finals).reshape(quads, heads, 128, 128)
     entering, _ = lax.optimization_barrier((entering, finals))
-    mixed = finish(doc_lengths, queries, keys, values, entering, local, gate, gain, crow, ccol)
-    owned = pick_owned((flags[0] // members).reshape(1), flags[1].reshape(1), arrived, rest)
-    return mixed, owned
+    mixed = finish(doc_lengths, queries, flipped, values, entering, local1, local2, gate, gain, crow, ccol)
+    arrived = lax.dynamic_slice(arrived, (flags[0], 0, 0, 0), (1, heads, 128, 128))
+    return mixed, jnp.where(flags[1] > 0, rest, arrived)
 
 
 def solution(mesh):

time: 94.5 us -> 120 us (1.27)
  Pallas kernels: 52.6 us -> 70.2 us
  waiting for transfers between devices: 10.6 us -> 18.8 us
  local copies, waits for them, and re-layouts: 3.92 us -> 2.61 us
    pallas_call x4, Pallas kernels: 32.5 us -> 51.7 us  [the longest x1 27.6 us: finish(): pl.pallas_call(finish_kernel, grid=(heads // 2,), in_specs=[SMEM, wide, p...]
    ppermute x1 -> x4, waiting for transfers between devices: 4.75 us -> 18.8 us  [the longest x3 15.7 us: on_device(): lax.ppermute(entering[x], 'seq', [(s, s ^ x) for s in range(spread)])]
    all_to_all x4 -> x3, waiting for transfers between devices: 5.85 us -> 0.01 us  [swap(): lax.all_to_all(x, 'seq', split_axis=0, concat_axis=0, axis_index_groups=g...]
    ppermute x1 -> x4, starting transfers between devices: 4.47 us -> 7.99 us  [the longest x1 4.48 us: on_device(): coming = [lax.ppermute(leaving, 'seq', onward)]]
    all_to_all x4 -> x3, starting transfers between devices: 18.3 us -> 15.5 us  [swap(): lax.all_to_all(x, 'seq', split_axis=0, concat_axis=0, axis_index_groups=g...]
    pallas_call x1, Pallas kernels: 2.02 us -> 0.73 us  [enter_states(): pl.pallas_call(functools.partial(enter_kernel, rows), in_specs=[SMEM, VME...]
  transfers between devices with their start and end apart: 5 -> 7, of which waited for: 3 -> 4; matrix products, arithmetic and copies ran while one was open for 1% -> 1% of each run, Pallas kernels for 44% -> 50%
where the time goes in v4:
time: 120 us
  Pallas kernels  70.2 us (58%)
  starting transfers between devices  23.5 us (20%)
  waiting for transfers between devices  18.8 us (16%)
  between operations  3.79 us (3%)
  local copies, waits for them, and re-layouts  2.61 us (2%)
    pallas_call x1, Pallas kernels, finish(): pl.pallas_call(finish_kernel, grid=(heads // 2,), in_specs=[SMEM, wide, p...  27.6 us
    pallas_call x2, Pallas kernels, early_attention(): pl.pallas_call(functools.partial(early_kernel, skip), grid=(EARLY // 2,),...  23.4 us
    ppermute x3, waiting for transfers between devices, on_device(): lax.ppermute(entering[x], 'seq', [(s, s ^ x) for s in range(spread)])  15.7 us
    all_to_all x3, starting transfers between devices, swap(): lax.all_to_all(x, 'seq', split_axis=0, concat_axis=0, axis_index_groups=g...  15.5 us
    pallas_call x1, Pallas kernels, side_pieces(): pl.pallas_call(functools.partial(side_kernel, slots, by_owner), grid=(mem...  8.27 us
    pallas_call x1, Pallas kernels, last_pieces(): pl.pallas_call(last_kernel, grid=(members,), in_specs=[SMEM, whole((heads...  7.34 us
    ppermute x1, starting transfers between devices, on_device(): coming = [lax.ppermute(leaving, 'seq', onward)]  4.48 us
    ppermute x3, starting transfers between devices, on_device(): lax.ppermute(entering[x], 'seq', [(s, s ^ x) for s in range(spread)])  3.51 us
  transfers between devices with their start and end apart: 7, of which 4 were waited for; matrix products, arithmetic and copies ran while one was open for 1% of the time, Pallas kernels for 50%

profile of v4, /device:TPU:0, one launch (start us, length us, event | category | flops | bytes accessed | tf_op | source)
XLA Modules:
  0.0 119.7 jit_solution(10024528882240119155)
XLA Ops:
  0.6 0.0 copy-start.1
  0.6 0.0 copy-start.5
  0.7 0.0 copy-start.7
  0.7 7.3 %last_pieces.1 = (bf16[4,528,128]{2,1,0:T(8,128)(2,1)}, f32[16,1024]{1,0:T(8,128)S(1)}, bf16[2048,1024]{1,0:T(8,128)(2,1)}) custom-call(s32[8]{0:T(128)} %len_ref.15, f32[16,1024]{1,0:T(8,128)} %bitcast.7, bf16[1024,2048]{1,0:T(8,128)(2,1)} %k_ref.1, bf16[1024,2048]{1,0:T(8,128)(2,1)} %v_ref.9), custom_call_target="tpu_custom_call" | custom-call | flops 536870912 | bytes 12582912 | tf_op jit(solution)/shard_map/last_pieces/pallas_call | solution.py:130
  8.0 5.2 %all-to-all-start.1 = ((bf16[4,528,128]{2,1,0:T(8,128)(2,1)}), bf16[4,528,128]{2,1,0:T(8,128)(2,1)S(1)}, u32[]{:S(2)}, u32[]{:S(2)}) async-start(bf16[4,528,128]{2,1,0:T(8,128)(2,1)} %get-tuple-element.56), calls=%async_computation.1 | async-start | bytes 1081344 | tf_op jit(solution)/shard_map/all_to_all | solution.py:555
  13.2 0.0 copy-done.1
  13.2 0.0 copy-done.5
  13.3 0.0 copy-done.7
  13.3 8.3 %side_pieces.3 = (bf16[4,1536,128]{2,1,0:T(8,128)(2,1)}, f32[1024,16]{1,0:T(8,128)}, s32[4]{0:T(128)S(1)}) custom-call(s32[8]{0:T(128)S(1)} %copy-done.5, s32[8]{0:T(128)S(1)} %copy-done.7, f32[16,1024]{1,0:T(8,128)S(1)} %bitcast.8, f32[16,1024]{1,0:T(8,128)S(1)} %get-tuple-element.73.crow_ref, bf16[2048,1024]{1,0:T(8,128)(2,1)} %get-tuple-element.55.kt_ref, ...), custom_call_target="tpu_custom_call" | custom-call | flops 1610612736 | bytes 8388608 | tf_op jit(solution)/shard_map/side_pieces/pallas_call | solution.py:233
  21.5 0.6 fusion
  22.7 0.0 all-to-all-done.1.last_ref
  22.7 0.7 leave_quad.1
  23.4 0.1 conditional.1
  23.4 0.1 broadcast.2
  23.6 4.2 %all-to-all-start.2 = ((bf16[4,1536,128]{2,1,0:T(8,128)(2,1)}), bf16[4,1536,128]{2,1,0:T(8,128)(2,1)S(1)}, u32[]{:S(2)}, u32[]{:S(2)}) async-start(bf16[4,1536,128]{2,1,0:T(8,128)(2,1)} %get-tuple-element.72), calls=%async_computation.2 | async-start | bytes 3145728 | tf_op jit(solution)/shard_map/all_to_all | solution.py:555
  27.8 4.5 %collective-permute-start = (bf16[4,128,128]{2,1,0:T(8,128)(2,1)S(1)}, bf16[4,128,128]{2,1,0:T(8,128)(2,1)S(1)}, u32[]{:S(2)}, u32[]{:S(2)}) collective-permute-start(bf16[4,128,128]{2,1,0:T(8,128)(2,1)S(1)} %leave_quad.1), channel_id=1, source_target_pairs={{0,8},{2,10},{4,12},{6,14},{1,9},{3,11},{5,13},{7,15},{16,24},{18,... | collective-permute-start | bytes 393224 | tf_op jit(solution)/shard_map/ppermute | solution.py:574
  32.3 11.7 %early_attention.2.local1_ref = f32[1024,512]{1,0:T(8,128)} custom-call(s32[8]{0:T(128)S(1)} %copy-done.5, bf16[1024,2048]{1,0:T(8,128)(2,1)} %q_ref.5, bf16[2048,1024]{1,0:T(8,128)(2,1)} %get-tuple-element.55.kt_ref, bf16[1024,2048]{1,0:T(8,128)(2,1)} %v_ref.9, f32[16,1024]{1,0:T(8,128)S(1)} %get-tuple-element.73.crow_ref, ...), custom_call_target="tpu_custom_call" | custom-call | flops 536870912 | bytes 5242880 | tf_op jit(solution)/shard_map/early_attention/pallas_call | solution.py:322
  44.0 3.1 %collective-permute-done.in_ref = bf16[4,128,128]{2,1,0:T(8,128)(2,1)S(1)} collective-permute-done((bf16[4,128,128]{2,1,0:T(8,128)(2,1)S(1)}, bf16[4,128,128]{2,1,0:T(8,128)(2,1)S(1)}, u32[]{:S(2)}, u32[]{:S(2)}) %collective-permute-start) | collective-permute-done | bytes 131104 | tf_op jit(solution)/shard_map/ppermute | solution.py:574
  47.1 0.7 enter_states.1
  47.8 0.0 copy-start
  47.8 0.6 copy-done
  48.4 11.7 %early_attention.3.local2_ref = f32[1024,512]{1,0:T(8,128)} custom-call(s32[8]{0:T(128)S(1)} %copy-done.5, bf16[1024,2048]{1,0:T(8,128)(2,1)} %q_ref.5, bf16[2048,1024]{1,0:T(8,128)(2,1)} %get-tuple-element.55.kt_ref, bf16[1024,2048]{1,0:T(8,128)(2,1)} %v_ref.9, f32[16,1024]{1,0:T(8,128)S(1)} %get-tuple-element.73.crow_ref, ...), custom_call_target="tpu_custom_call" | custom-call | flops 536870912 | bytes 5242880 | tf_op jit(solution)/shard_map/early_attention/pallas_call | solution.py:322
  60.2 0.0 copy-start.6
  60.2 0.0 all-to-all-done.2.side_ref
  60.2 2.1 %final_states.1 = bf16[8,4,128,128]{3,2,1,0:T(8,128)(2,1)} custom-call(s32[8]{0:T(128)S(1)} %copy-done.5, s32[8]{0:T(128)S(1)} %copy-done.7, bf16[4,528,128]{2,1,0:T(8,128)(2,1)S(1)} %all-to-all-done.1.last_ref, bf16[4,1536,128]{2,1,0:T(8,128)(2,1)S(1)} %all-to-all-done.2.side_ref, bf16[4,128,128]{2,1,0:T(8,128)(2,1)S(1)} %collective-permute-done.in_ref), custom_call_target="tpu_custom_call" | custom-call | tf_op jit(solution)/shard_map/final_states/pallas_call | solution.py:451
  62.3 6.1 %all-to-all-start.3 = ((bf16[8,4,128,128]{3,2,1,0:T(8,128)(2,1)}), bf16[8,4,128,128]{3,2,1,0:T(8,128)(2,1)S(1)}, u32[]{:S(2)}, u32[]{:S(2)}) async-start(bf16[8,4,128,128]{3,2,1,0:T(8,128)(2,1)} %final_states.1), calls=%async_computation.3 | async-start | bytes 2097152 | tf_op jit(solution)/shard_map/all_to_all | solution.py:555
  68.4 2.0 %collective-permute-start.1 = (bf16[4,128,128]{2,1,0:T(8,128)(2,1)S(1)}, bf16[4,128,128]{2,1,0:T(8,128)(2,1)S(1)}, u32[]{:S(2)}, u32[]{:S(2)}) collective-permute-start(bf16[4,128,128]{2,1,0:T(8,128)(2,1)S(1)} %get-tuple-element.69), channel_id=1, source_target_pairs={{0,2},{2,0},{4,6},{6,4},{8,10},{10,8},{12,14},{14,12},{1,3},{3,1},... | collective-permute-start | bytes 393224 | tf_op jit(solution)/shard_map/ppermute | solution.py:589
  70.4 1.5 %collective-permute-start.2 = (bf16[4,128,128]{2,1,0:T(8,128)(2,1)S(1)}, bf16[4,128,128]{2,1,0:T(8,128)(2,1)S(1)}, u32[]{:S(2)}, u32[]{:S(2)}) collective-permute-start(bf16[4,128,128]{2,1,0:T(8,128)(2,1)S(1)} %get-tuple-element.70), channel_id=1, source_target_pairs={{0,4},{2,6},{4,0},{6,2},{8,12},{10,14},{12,8},{14,10},{1,5},{3,7},... | collective-permute-start | bytes 393224 | tf_op jit(solution)/shard_map/ppermute | solution.py:589
  71.9 0.0 collective-permute-start.3
  73.7 0.0 copy-done.6
  73.8 0.6 reshape.16.gain_ref
  75.0 3.1 %collective-permute-done.1.e1 = bf16[4,128,128]{2,1,0:T(8,128)(2,1)S(1)} collective-permute-done((bf16[4,128,128]{2,1,0:T(8,128)(2,1)S(1)}, bf16[4,128,128]{2,1,0:T(8,128)(2,1)S(1)}, u32[]{:S(2)}, u32[]{:S(2)}) %collective-permute-start.1) | collective-permute-done | bytes 131104 | tf_op jit(solution)/shard_map/ppermute | solution.py:589
  78.0 0.0 copy-start.2
  78.0 10.1 %collective-permute-done.2.e2 = bf16[4,128,128]{2,1,0:T(8,128)(2,1)S(1)} collective-permute-done((bf16[4,128,128]{2,1,0:T(8,128)(2,1)S(1)}, bf16[4,128,128]{2,1,0:T(8,128)(2,1)S(1)}, u32[]{:S(2)}, u32[]{:S(2)}) %collective-permute-start.2) | collective-permute-done | bytes 131104 | tf_op jit(solution)/shard_map/ppermute | solution.py:589
  88.1 0.0 copy-start.3
  88.1 2.5 %collective-permute-done.3.e3 = bf16[4,128,128]{2,1,0:T(8,128)(2,1)S(1)} collective-permute-done((bf16[4,128,128]{2,1,0:T(8,128)(2,1)S(1)}, bf16[4,128,128]{2,1,0:T(8,128)(2,1)S(1)}, u32[]{:S(2)}, u32[]{:S(2)}) %collective-permute-start.3) | collective-permute-done | bytes 131104 | tf_op jit(solution)/shard_map/ppermute | solution.py:589
  90.7 0.0 copy-done.2
  90.7 0.0 copy-done.3
  90.7 0.0 copy-start.4
  90.7 0.7 copy-done.4
  91.3 27.6 %finish.1 = bf16[1024,2048]{1,0:T(8,128)(2,1)} custom-call(s32[8]{0:T(128)S(1)} %copy-done.5, bf16[1024,2048]{1,0:T(8,128)(2,1)} %q_ref.5, bf16[2048,1024]{1,0:T(8,128)(2,1)} %get-tuple-element.55.kt_ref, bf16[1024,2048]{1,0:T(8,128)(2,1)} %v_ref.9, bf16[4,128,128]{2,1,0:T(8,128)(2,1)} %copy-done, bf16[4,128,128]{2,1,0:T(8,128)(2,1)} %copy-done.2, ...), custom_call_target="tpu_custom_call" | custom-call | flops 2147483648 | bytes 20971520 | tf_op jit(solution)/shard_map/finish/pallas_call | solution.py:525
  118.9 0.0 all-to-all-done.3
  118.9 0.9 dynamic-slice_select_fusion
Async XLA Ops:
  0.6 12.6 %copy-start.1 = (f32[1024,16]{0,1:T(8,128)S(1)}, f32[1024,16]{0,1:T(8,128)}, u32[]{:S(2)}) copy-start(f32[1024,16]{0,1:T(8,128)} %param.13) | copy-start | bytes 196612
  0.6 12.6 %copy-start.5 = (s32[8]{0:T(128)S(1)}, s32[8]{0:T(128)}, u32[]{:S(2)}) copy-start(s32[8]{0:T(128)} %len_ref.15) | copy-start | bytes 100
  0.7 12.6 %copy-start.7 = (s32[8]{0:T(128)S(1)}, s32[8]{0:T(128)}, u32[]{:S(2)}) copy-start(s32[8]{0:T(128)} %own_ref.3) | copy-start | bytes 100
  8.0 14.7 %all-to-all-start.1 = ((bf16[4,528,128]{2,1,0:T(8,128)(2,1)}), bf16[4,528,128]{2,1,0:T(8,128)(2,1)S(1)}, u32[]{:S(2)}, u32[]{:S(2)}) async-start(bf16[4,528,128]{2,1,0:T(8,128)(2,1)} %get-tuple-element.56), calls=%async_computation.1 | async-start | bytes 1081344 | tf_op jit(solution)/shard_map/all_to_all | solution.py:555
  23.6 36.6 %all-to-all-start.2 = ((bf16[4,1536,128]{2,1,0:T(8,128)(2,1)}), bf16[4,1536,128]{2,1,0:T(8,128)(2,1)S(1)}, u32[]{:S(2)}, u32[]{:S(2)}) async-start(bf16[4,1536,128]{2,1,0:T(8,128)(2,1)} %get-tuple-element.72), calls=%async_computation.2 | async-start | bytes 3145728 | tf_op jit(solution)/shard_map/all_to_all | solution.py:555
  27.8 19.3 %collective-permute-start = (bf16[4,128,128]{2,1,0:T(8,128)(2,1)S(1)}, bf16[4,128,128]{2,1,0:T(8,128)(2,1)S(1)}, u32[]{:S(2)}, u32[]{:S(2)}) collective-permute-start(bf16[4,128,128]{2,1,0:T(8,128)(2,1)S(1)} %leave_quad.1), channel_id=1, source_target_pairs={{0,8},{2,10},{4,12},{6,14},{1,9},{3,11},{5,13},{7,15},{16,24},{18,... | collective-permute-start | bytes 393224 | tf_op jit(solution)/shard_map/ppermute | solution.py:574
  47.8 0.6 copy-start
  60.2 13.6 %copy-start.6 = (bf16[2048]{0:T(1024)(128)(2,1)S(1)}, bf16[2048]{0:T(1024)(128)(2,1)}, u32[]{:S(2)}) copy-start(bf16[2048]{0:T(1024)(128)(2,1)} %param.15) | copy-start | bytes 12292
  62.3 56.6 %all-to-all-start.3 = ((bf16[8,4,128,128]{3,2,1,0:T(8,128)(2,1)}), bf16[8,4,128,128]{3,2,1,0:T(8,128)(2,1)S(1)}, u32[]{:S(2)}, u32[]{:S(2)}) async-start(bf16[8,4,128,128]{3,2,1,0:T(8,128)(2,1)} %final_states.1), calls=%async_computation.3 | async-start | bytes 2097152 | tf_op jit(solution)/shard_map/all_to_all | solution.py:555
  68.4 9.7 %collective-permute-start.1 = (bf16[4,128,128]{2,1,0:T(8,128)(2,1)S(1)}, bf16[4,128,128]{2,1,0:T(8,128)(2,1)S(1)}, u32[]{:S(2)}, u32[]{:S(2)}) collective-permute-start(bf16[4,128,128]{2,1,0:T(8,128)(2,1)S(1)} %get-tuple-element.69), channel_id=1, source_target_pairs={{0,2},{2,0},{4,6},{6,4},{8,10},{10,8},{12,14},{14,12},{1,3},{3,1},... | collective-permute-start | bytes 393224 | tf_op jit(solution)/shard_map/ppermute | solution.py:589
  70.4 17.7 %collective-permute-start.2 = (bf16[4,128,128]{2,1,0:T(8,128)(2,1)S(1)}, bf16[4,128,128]{2,1,0:T(8,128)(2,1)S(1)}, u32[]{:S(2)}, u32[]{:S(2)}) collective-permute-start(bf16[4,128,128]{2,1,0:T(8,128)(2,1)S(1)} %get-tuple-element.70), channel_id=1, source_target_pairs={{0,4},{2,6},{4,0},{6,2},{8,12},{10,14},{12,8},{14,10},{1,5},{3,7},... | collective-permute-start | bytes 393224 | tf_op jit(solution)/shard_map/ppermute | solution.py:589
  71.9 18.8 %collective-permute-start.3 = (bf16[4,128,128]{2,1,0:T(8,128)(2,1)S(1)}, bf16[4,128,128]{2,1,0:T(8,128)(2,1)S(1)}, u32[]{:S(2)}, u32[]{:S(2)}) collective-permute-start(bf16[4,128,128]{2,1,0:T(8,128)(2,1)S(1)} %get-tuple-element.71), channel_id=1, source_target_pairs={{0,6},{2,4},{4,2},{6,0},{8,14},{10,12},{12,10},{14,8},{1,7},{3,5},... | collective-permute-start | bytes 393224 | tf_op jit(solution)/shard_map/ppermute | solution.py:589
  78.0 12.6 %copy-start.2 = (bf16[4,128,128]{2,1,0:T(8,128)(2,1)}, bf16[4,128,128]{2,1,0:T(8,128)(2,1)S(1)}, u32[]{:S(2)}) copy-start(bf16[4,128,128]{2,1,0:T(8,128)(2,1)S(1)} %collective-permute-done.1.e1) | copy-start | bytes 393220
  88.1 2.5 %copy-start.3 = (bf16[4,128,128]{2,1,0:T(8,128)(2,1)}, bf16[4,128,128]{2,1,0:T(8,128)(2,1)S(1)}, u32[]{:S(2)}) copy-start(bf16[4,128,128]{2,1,0:T(8,128)(2,1)S(1)} %collective-permute-done.2.e2) | copy-start | bytes 393220
  90.7 0.7 copy-start.4
